TPU v7x, 32 devices: a whole 2x2x4 slice. The times are simulated.
32 devices in a mesh: section: 2 (over x), batch: 16 (over z, y, core).
Axes of the slice: x: 2, y: 2, z: 4, core: 2. Of those that a mesh axis runs over, the one named last changes fastest.
Arguments:
- inputs: bfloat16 [9216, 768], P('batch', 'section'), may hold values from -6 to 6
- seq_lengths: int32 [16, 8], P('batch'), may hold values from 0 to 576, as said below
- cotangent: bfloat16 [9216, 768], P('batch', 'section'), may hold values from -6 to 6
- first_gain: float32 [768], replicated, may hold values from 0.25 to 1.75
- first_bias: float32 [768], replicated, may hold values from -2 to 2
- joint_weight: bfloat16 [768, 2304], replicated, may hold values from -0.21875 to 0.21875
- query_bias: float32 [768], replicated, may hold values from -2 to 2
- value_bias: float32 [768], replicated, may hold values from -2 to 2
- second_gain: float32 [768], replicated, may hold values from 0.25 to 1.75
- second_bias: float32 [768], replicated, may hold values from -2 to 2
- output_weight: bfloat16 [768, 768], replicated, may hold values from -0.21875 to 0.21875
- output_bias: float32 [768], replicated, may hold values from -2 to 2
- third_gain: float32 [768], replicated, may hold values from 0.25 to 1.75
- third_bias: float32 [768], replicated, may hold values from -2 to 2
- inner_weight: bfloat16 [768, 3072], replicated, may hold values from -0.21875 to 0.21875
- inner_bias: float32 [3072], replicated, may hold values from -2 to 2
- fourth_gain: float32 [3072], replicated, may hold values from 0.25 to 1.75
- fourth_bias: float32 [3072], replicated, may hold values from -2 to 2
- down_weight: bfloat16 [3072, 768], replicated, may hold values from -0.109375 to 0.109375
- down_bias: float32 [768], replicated, may hold values from -2 to 2
Outputs:
- result: bfloat16 [9216, 768], P('batch', 'section')
- input_grad: bfloat16 [9216, 768], P('batch', 'section')
- first_gain_grad: float32 [768], P('section')
- first_bias_grad: float32 [768], P('section')
- joint_weight_grad: float32 [768, 2304], P('section')
- query_bias_grad: float32 [768], P('section')
- value_bias_grad: float32 [768], P('section')
- second_gain_grad: float32 [768], P('section')
- second_bias_grad: float32 [768], P('section')
- output_weight_grad: float32 [768, 768], P('section')
- output_bias_grad: float32 [768], P('section')
- third_gain_grad: float32 [768], P('section')
- third_bias_grad: float32 [768], P('section')
- inner_weight_grad: float32 [768, 3072], P('section')
- inner_bias_grad: float32 [3072], P('section')
- fourth_gain_grad: float32 [3072], P('section')
- fourth_bias_grad: float32 [3072], P('section')
- down_weight_grad: float32 [3072, 768], P('section')
- down_bias_grad: float32 [768], P('section')
Inputs may be any that keep to these rules, and one draw needn't show every extreme that they name: `seq_lengths`: row b lists the lengths of the sequences packed one after another from the first of the 576 token slots of batch index b; a row sums to at most 576, the slots after that sum are padding, and a zero marks an unused sequence slot. In every draw some batch index holds one sequence that fills all 576 slots.
All inputs are finite; a program needn't handle non-finite values.
Results may differ from a plain program's by a relative error of at most 0.012.
Values may be sent and summed in bfloat16 or wider, within the bound.
A program may use at most 192 MiB of HBM per device.

v0:
```python
import functools

import jax
import jax.numpy as jnp
from jax import lax
from jax.experimental import pallas as pl
from jax.experimental.pallas import tpu as pltpu
from jax.sharding import PartitionSpec as P

HEADS = 12
EPSILON = 1e-05
MASKED = -1e9
F32 = jnp.float32
BF16 = jnp.bfloat16
MESH = pl.DeviceIdType.MESH
GROUP = 16
PAIRS = HEADS // 4
UNITS = 12
Y_FIRST = (1, 4, 7, 10)
Y_GATHER = (1, 3, 5, 7, 9, 11)
GELU_C = 0.7978845608028654
GELU_A = 0.044715


def gray(v):
    return v + (v // 2) * (1 - 2 * (v % 2))


def aligned(v, by):
    return pl.multiple_of(v, by)


def normal(values):
    average = jnp.mean(values, axis=-1, keepdims=True)
    centered = values - average
    spread = jnp.mean(centered * centered, axis=-1, keepdims=True)
    scale = lax.rsqrt(spread + EPSILON)
    return centered * scale, scale


def normal_back(vhat, scale, gain, grad):
    scaled = grad * gain
    first = jnp.mean(scaled, axis=-1, keepdims=True)
    second = jnp.mean(scaled * vhat, axis=-1, keepdims=True)
    return scale * (scaled - first - vhat * second)


def dot(left, right):
    return jnp.dot(left, right, preferred_element_type=F32)


def dot_t(left, right):
    return lax.dot_general(left, right, (((1,), (1,)), ((), ())), preferred_element_type=F32)


def t_dot(left, right):
    return lax.dot_general(left, right, (((0,), (0,)), ((), ())), preferred_element_type=F32)


def by8(values):
    rows = values.shape[0]
    return jnp.sum(values.reshape(rows // 8, 8, values.shape[1]), axis=0)


class Copies:
    def __init__(self, send, recv):
        self.send, self.recv, self.count, self.open = send, recv, 0, []

    def remote(self, src, dst, device):
        at = self.count
        self.count += 1
        return pltpu.make_async_remote_copy(
            src_ref=src,
            dst_ref=dst,
            send_sem=self.send.at[at],
            recv_sem=self.recv.at[at],
            device_id=device,
            device_id_type=MESH,
        )

    def go(self, src, dst, device):
        copy = self.remote(src, dst, device)
        copy.start()
        self.open.append(copy)
        return copy

    def drain(self):
        for copy in self.open:
            copy.wait_send()
        self.open = []


def layer_kernel(
    x_in, cot_in, lens, wj_in, wo_in, wi_in, wd_in,
    first_gain, first_bias, query_bias, value_bias, second_gain, second_bias, output_bias,
    third_gain, third_bias, inner_bias, fourth_gain, fourth_bias, down_bias,
    res_out, grad_out, gj_out, go_out, gi_out, gd_out, bv_out,
    wj, wo, wi, wd, feats, cots, ends, normed, q, k, v, vt, kt, bias, pt, mixed_own, mixed,
    sub, fn, handed, tmp, vh, dg, fs, fs_sib, gi_sib, up, gfn, hgr, hg_sib, gmix, do, dqkv,
    gn_sib, result, stat, cols, bv, bv_in, grads, r1, r2, rz, oy,
    lsem, ssem, rsem,
):
    R, HD = x_in.shape
    D = 2 * HD
    H = R // 2
    FF = wi.shape[1]
    T = 256
    NT = FF // T
    x = lax.axis_index("section")
    b = lax.axis_index("batch")
    base = (b // GROUP) * GROUP
    z, y, c = (b // 4) % 4, (b // 2) % 2, b % 2
    p = gray(z)

    def dev(x_, z_, y_, c_):
        return (x_, base + z_ * 4 + y_ * 2 + c_)

    sib = dev(x, z, y, 1 - c)
    xp = dev(1 - x, z, y, c)
    xc = dev(1 - x, z, y, 1 - c)
    yp = dev(x, z, 1 - y, c)
    nxt = dev(x, gray((p + 1) % 4), y, c)
    prv = dev(x, gray((p + 3) % 4), y, c)
    home = c == x
    away = c != x
    own = aligned(c * H, 32)
    other = aligned((1 - c) * H, 32)
    cp = Copies(ssem, rsem)
    local_count = [0]

    def local(src, dst):
        copy = pltpu.make_async_copy(src, dst, lsem.at[local_count[0]])
        local_count[0] += 1
        copy.start()
        return copy

    wj_copies = [local(wj_in.at[:, pl.ds(aligned(t * D + c * HD, 128), HD)], wj.at[t]) for t in range(3)]
    wo_copy = local(wo_in, wo)
    wi_copy = local(wi_in, wi)
    wd_copy = local(wd_in, wd)

    barrier = pltpu.get_barrier_semaphore()
    for peer in (sib, xp, xc, yp, nxt, prv):
        pl.semaphore_signal(barrier, inc=1, device_id=peer, device_id_type=MESH)
    pl.semaphore_wait(barrier, 6)

    NC = 3
    RC = R // NC
    c_native = [cp.remote(src, dst.at[x], sib) for src, dst in ((x_in, feats), (cot_in, cots))]
    c_ends = cp.remote(ends, ends, sib)
    c_cross = [
        cp.remote(x_in.at[pl.ds(i * RC, RC)], feats.at[x, pl.ds(i * RC, RC)], xp) for i in range(NC)
    ]
    c_pass = [
        cp.remote(feats.at[1 - x, pl.ds(i * RC, RC)], feats.at[1 - x, pl.ds(i * RC, RC)], sib)
        for i in range(NC)
    ]
    cot_cross = cp.remote(cot_in, cots.at[x], xp)
    cot_pass = cp.remote(cots.at[1 - x], cots.at[1 - x], sib)
    l_native = [
        pltpu.make_async_copy(src, dst.at[x], lsem.at[12 + i])
        for i, (src, dst) in enumerate(((x_in, feats), (cot_in, cots)))
    ]

    @pl.when(away)
    def _():
        for copy in c_cross:
            copy.start()
        cot_cross.start()

    @pl.when(home)
    def _():
        c_native[0].start()
        l_native[0].start()
        lane = lax.broadcasted_iota(jnp.int32, (1, 8), 1)
        lengths = lens[...].astype(F32)
        for j in range(8):
            end = jnp.sum(jnp.where(lane <= j, lengths, 0.0), axis=1, keepdims=True)
            ends[j : j + 1, :] = jnp.broadcast_to(end, (1, 128))
        c_ends.start()
        l_native[1].start()
        c_native[1].start()
        l_native[0].wait()

    @pl.when(away)
    def _():
        c_native[0].wait_recv()
        c_ends.wait_recv()

    zeros = jnp.zeros((640 - R, HD), BF16)
    for ref in (q, do):
        ref[R:640, :] = zeros

    key_at = lax.broadcasted_iota(jnp.int32, (R, 128), 0).astype(F32)
    key_segment = sum((key_at >= ends[j : j + 1, :]).astype(F32) for j in range(8))
    for j in range(5):
        query_at = (lax.broadcasted_iota(jnp.int32, (1, 128), 1) + j * 128).astype(F32)
        query_segment = sum((query_at >= ends[i : i + 1, :]).astype(F32) for i in range(8))
        allowed = (key_segment == query_segment) & (key_at <= query_at)
        bias[:, j * 128 : (j + 1) * 128] = jnp.where(allowed, 0.0, MASKED).astype(BF16)

    def feature_rows(at, count):
        return jnp.concatenate([feats[0, pl.ds(at, count)], feats[1, pl.ds(at, count)]], 1).astype(F32)

    for copy in wj_copies:
        copy.wait()
    heads_at = aligned(c * HD, 128)
    own_query_bias = query_bias[:, pl.ds(heads_at, HD)]
    own_value_bias = value_bias[:, pl.ds(heads_at, HD)]
    for i in range(NC):

        @pl.when(home)
        def _():
            c_cross[i].wait_recv()
            c_pass[i].start()

        @pl.when(away)
        def _():
            c_pass[i].wait_recv()

        @pl.loop(0, RC // 48)
        def _(step):
            at = aligned(i * RC + step * 48, 16)
            vhat, _ = normal(feature_rows(at, 48))
            normed[pl.ds(at, 48), :] = (vhat * first_gain[...] + first_bias[...]).astype(BF16)

        rows = normed[i * RC : (i + 1) * RC, :]
        at = pl.ds(i * RC, RC)
        q[at, :] = ((dot(rows, wj[0]) + own_query_bias).astype(BF16) * 0.125).astype(BF16)
        k[at, :] = dot(rows, wj[1]).astype(BF16)
        v[at, :] = (dot(rows, wj[2]) + own_value_bias).astype(BF16)
    vt[:, :R] = v[...].T

    first_half = lax.broadcasted_iota(jnp.int32, (128, 128), 1) < 64

    def split_pair(tile):
        zero = jnp.zeros_like(tile)
        return jnp.concatenate([jnp.where(first_half, tile, zero), jnp.where(first_half, zero, tile)], 0)

    blocks = []
    at = 0
    for j in range(5):
        blocks.append((j, min(128 * (j + 1), R), at))
        at += min(128 * (j + 1), R)
    for pr in range(PAIRS):
        lanes = slice(pr * 128, (pr + 1) * 128)
        for j, nk, at in blocks:
            qs = slice(j * 128, (j + 1) * 128)
            block_bias = bias[:nk, qs].astype(F32)
            scores = dot_t(k[:nk, lanes], split_pair(q[qs, lanes]))
            scores = scores + jnp.concatenate([block_bias, block_bias], 1)
            largest = jnp.max(scores, axis=0, keepdims=True)
            shifted = jnp.exp(scores - largest)
            summed = jnp.sum(shifted, axis=0, keepdims=True)
            probs = (shifted * (1.0 / summed)).astype(BF16)
            pt[pr, at : at + nk, :] = probs
            out = dot(vt[lanes, :nk], probs)
            mixed_own[qs, lanes] = jnp.concatenate([out[:64, :128], out[64:, 128:]], 0).T

    c_mixed = cp.go(
        mixed_own.at[pl.ds(other, H)], mixed.at[:, pl.ds(heads_at, HD)], sib
    )
    mixed[:, pl.ds(heads_at, HD)] = mixed_own[pl.ds(own, H), :]
    kt[:, :R] = k[...].T
    wo_copy.wait()
    c_mixed.wait_recv()
    own_live = (lax.broadcasted_iota(jnp.int32, (H, 1), 0) + c * H).astype(F32) < ends[7:8, 0:1]

    @pl.loop(0, H // 48)
    def _(step):
        at = aligned(step * 48, 16)
        vhat, _ = normal(mixed[pl.ds(at, 48), :])
        sub[pl.ds(own + at, 48), :] = (vhat * second_gain[...] + second_bias[...]).astype(BF16)

    branch = dot(sub[pl.ds(own, H), :], wo[...])
    for i in range(6):
        piece = slice(i * 48, (i + 1) * 48)
        handed[piece, :] = (
            feature_rows(own + i * 48, 48) + (branch[piece] + output_bias[...])
        ).astype(BF16)
        vhat, _ = normal(handed[piece, :].astype(F32))
        fn[pl.ds(own + i * 48, 48), :] = (vhat * third_gain[...] + third_bias[...]).astype(BF16)
    c_sub = cp.go(sub.at[pl.ds(own, H)], sub.at[pl.ds(own, H)], sib)
    c_fn = cp.go(fn.at[pl.ds(own, H)], fn.at[pl.ds(own, H)], sib)

    wi_copy.wait()
    stat[0] = jnp.zeros((H, 128), F32)

    @pl.loop(0, NT)
    def _(tile):
        at = pl.ds(aligned(tile * T, T), T)
        inner = dot(fn[pl.ds(own, H), :], wi[:, at])
        for i in range(9):
            piece = slice(i * 32, (i + 1) * 32)
            u = inner[piece] + inner_bias[:, at]
            square = u * u
            t = jnp.tanh(u * (GELU_C + (GELU_C * GELU_A) * square))
            half = 0.5 * u
            act = half + half * t
            tmp[piece, at] = act
            dg[piece, at] = (
                0.5 + 0.5 * t + (half - half * t * t) * (GELU_C + (3 * GELU_C * GELU_A) * square)
            ).astype(BF16)
            stat[0, piece, :] += act[:, :128] + act[:, 128:]

    mean = jnp.sum(stat[0], axis=1, keepdims=True) * (1.0 / FF)
    stat[1] = jnp.broadcast_to(mean, (H, 128))
    stat[0] = jnp.zeros((H, 128), F32)

    @pl.loop(0, NT)
    def _(tile):
        at = pl.ds(aligned(tile * T, T), T)
        for i in range(9):
            piece = slice(i * 32, (i + 1) * 32)
            m = stat[1, piece, :]
            cen = tmp[piece, at] - jnp.concatenate([m, m], 1)
            sq = cen * cen
            stat[0, piece, :] += sq[:, :128] + sq[:, 128:]

    spread = jnp.sum(stat[0], axis=1, keepdims=True) * (1.0 / FF)
    stat[2] = jnp.broadcast_to(lax.rsqrt(spread + EPSILON), (H, 128))

    @pl.loop(0, NT)
    def _(tile):
        at = pl.ds(aligned(tile * T, T), T)
        for i in range(9):
            piece = slice(i * 32, (i + 1) * 32)
            m, s = stat[1, piece, :], stat[2, piece, :]
            vhat = (tmp[piece, at] - jnp.concatenate([m, m], 1)) * jnp.concatenate([s, s], 1)
            vh[piece, at] = vhat.astype(BF16)
            fs[piece, at] = (vhat * fourth_gain[:, at] + fourth_bias[:, at]).astype(BF16)

    c_fs = [
        cp.go(
            fs.at[:, pl.ds(aligned((2 * i + 1 - c) * D, 128), D)],
            fs_sib.at[:, i * D : (i + 1) * D],
            sib,
        )
        for i in range(2)
    ]

    @pl.when(home)
    def _():
        cot_cross.wait_recv()
        cot_pass.start()
        l_native[1].wait()
        cot_pass.wait_send()

    @pl.when(away)
    def _():
        c_native[1].wait_recv()
        cot_pass.wait_recv()

    @pl.loop(0, R // 48)
    def _(step):
        at = aligned(step * 48, 16)
        alive = (lax.broadcasted_iota(jnp.int32, (48, 1), 0) + at).astype(F32) < ends[7:8, 0:1]
        for h in range(2):
            rows = cots[h, pl.ds(at, 48), :].astype(F32)
            cots[h, pl.ds(at, 48), :] = jnp.where(alive, rows, 0.0).astype(BF16)

    up[:, :HD] = cots[0, pl.ds(own, H), :]
    up[:, HD:] = cots[1, pl.ds(own, H), :]

    events = []

    def units(first, count, left_own, left_sib, right):
        for i in range(count):
            for h in range(2):
                rows = jnp.concatenate([left_own(i, h), left_sib(i, h)], 0)
                grads[first + i, h] = t_dot(rows, right(i)).astype(BF16)
            send_unit(first + i)

    copies = {}
    half_rows = HD // 2
    piece_rows = HD // 8

    def y_rows(y_):
        return pl.ds(aligned(y_ * half_rows, 32), half_rows)

    def z_rows(piece, y_=None):
        y_ = y if y_ is None else y_
        return pl.ds(aligned(y_ * half_rows + piece * piece_rows, 16), piece_rows)

    def add(dst, rows, src, src_rows):
        dst[rows, :] = (dst[rows, :].astype(F32) + src[src_rows, :].astype(F32)).astype(BF16)

    def send_unit(u):
        if u in Y_FIRST:
            for h in range(2):
                copies[u, "a", h] = cp.go(
                    grads.at[u, h, y_rows(1 - y)], r1.at[u, h * half_rows : (h + 1) * half_rows], yp
                )
        else:
            copies[u, "a"] = cp.go(grads.at[u, 1 - x], r1.at[u], xp)

    def second(u):
        mine = grads.at[u, x]
        if u in Y_FIRST:
            for h in range(2):
                copies[u, "a", h].wait_recv()
            theirs = grads.at[u, 1 - x]
            add(theirs, y_rows(y), r1.at[u], y_rows(1 - x))
            copies[u, "b"] = cp.go(theirs.at[y_rows(y)], r2.at[u], xp)
            add(mine, y_rows(y), r1.at[u], y_rows(x))
        else:
            copies[u, "a"].wait_recv()
            add(mine, y_rows(1 - y), r1.at[u], y_rows(1 - y))
            copies[u, "b"] = cp.go(mine.at[y_rows(1 - y)], r2.at[u], yp)
            add(mine, y_rows(y), r1.at[u], y_rows(y))

    def third(u):
        mine = grads.at[u, x]
        copies[u, "b"].wait_recv()
        for s in range(4):
            piece = (p + 3 - s) % 4
            add(mine, z_rows(piece), r2.at[u], pl.ds(aligned(piece * piece_rows, 16), piece_rows))
            if s == 0:
                copies[u, "z", 0] = cp.go(mine.at[z_rows(piece)], rz.at[u, 0], nxt)

    def whole(u):
        return oy.at[Y_FIRST.index(u)] if u in Y_FIRST else r1.at[u]

    def ring(u, s):
        mine = grads.at[u, x]
        copies[u, "z", s].wait_recv()
        piece = (p + 2 - s) % 4
        if s < 2:
            add(mine, z_rows(piece), rz.at[u, s], pl.ds(0, piece_rows))
            copies[u, "z", s + 1] = cp.go(mine.at[z_rows(piece)], rz.at[u, s + 1], nxt)
        else:
            out = whole(u)
            out[z_rows(p), :] = (
                mine[z_rows(p), :].astype(F32) + rz[u, 2].astype(F32)
            ).astype(BF16)
            if u in Y_GATHER:
                copies[u, "gy"] = cp.go(out.at[z_rows(p)], out.at[z_rows(p)], yp)
            else:
                copies[u, "gz", 0] = [cp.go(out.at[z_rows(p)], out.at[z_rows(p)], nxt)]

    def gather_z(u, s):
        out = whole(u)
        for copy in copies[u, "gz", s]:
            copy.wait_recv()
        piece = (p + 3 - s) % 4
        sides = (0, 1) if u in Y_GATHER else (y,)
        if s < 2:
            copies[u, "gz", s + 1] = [
                cp.go(out.at[z_rows(piece, side)], out.at[z_rows(piece, side)], nxt)
                for side in sides
            ]
        elif u in Y_GATHER:
            deliver(u)
        else:
            copies[u, "gy"] = cp.go(out.at[y_rows(y)], out.at[y_rows(y)], yp)

    def gather_y(u):
        copies[u, "gy"].wait_recv()
        out = whole(u)
        if u in Y_GATHER:
            copies[u, "gz", 0] = [
                cp.go(out.at[z_rows(p, side)], out.at[z_rows(p, side)], nxt) for side in (0, 1)
            ]
        else:
            deliver(u)

    deliveries = []

    def deliver(u):
        if u < 4:
            target = gd_out.at[pl.ds(aligned(c * D + (u // 2) * HD, 128), HD), (u % 2) * HD : (u % 2 + 1) * HD]
        elif u < 8:
            target = gi_out.at[:, pl.ds(aligned(c * (FF // 2) + (u - 4) * HD, 128), HD)]
        elif u == 8:
            target = go_out.at[:, pl.ds(heads_at, HD)]
        else:
            target = gj_out.at[:, pl.ds(aligned((u - 9) * D + c * HD, 128), HD)]
        copy = cp.go(whole(u), target, sib)
        deliveries.append((copy, local(whole(u), target)))

    def steps_of(u):
        steps = [functools.partial(second, u), functools.partial(third, u)]
        steps += [functools.partial(ring, u, s) for s in range(3)]
        gather = [functools.partial(gather_z, u, s) for s in range(3)]
        if u in Y_GATHER:
            return steps + [functools.partial(gather_y, u)] + gather
        return steps + gather + [functools.partial(gather_y, u)]

    for copy in c_fs:
        copy.wait_recv()
    units(
        0, 4,
        lambda i, h: fs[:, pl.ds(aligned((2 * h + c) * D + (i // 2) * HD, 128), HD)],
        lambda i, h: fs_sib[:, h * D + (i // 2) * HD : h * D + (i // 2 + 1) * HD],
        lambda i: jnp.concatenate([cots[i % 2, pl.ds(own, H), :], cots[i % 2, pl.ds(other, H), :]], 0),
    )

    wd_copy.wait()
    c_result = [
        cp.remote(result.at[0, x], res_out.at[pl.ds(own, H)], sib),
        cp.remote(result.at[0, 1 - x], res_out.at[pl.ds(own, H)], xp),
        cp.remote(result.at[0, 1 - x], res_out.at[pl.ds(own, H)], xc),
        cp.remote(result.at[1, x], grad_out.at[pl.ds(own, H)], sib),
        cp.remote(result.at[1, 1 - x], grad_out.at[pl.ds(own, H)], xp),
        cp.remote(result.at[1, 1 - x], grad_out.at[pl.ds(own, H)], xc),
    ]
    l_result = [
        pltpu.make_async_copy(result.at[i, x], o.at[pl.ds(own, H)], lsem.at[14 + i])
        for i, o in enumerate((res_out, grad_out))
    ]

    def hand_out(i):
        @pl.when(home)
        def _():
            l_result[i].start()
            c_result[3 * i + 1].start()

        @pl.when(away)
        def _():
            c_result[3 * i].start()
            c_result[3 * i + 2].start()

    def handed_out(i):
        @pl.when(home)
        def _():
            l_result[i].wait()
            c_result[3 * i + 1].wait_send()
            c_result[3 * i].wait_recv()

        @pl.when(away)
        def _():
            c_result[3 * i].wait_send()
            c_result[3 * i + 2].wait_send()
            c_result[3 * i + 1].wait_recv()
            c_result[3 * i + 2].wait_recv()

    branch = dot(fs[...], wd[...])
    for i in range(6):
        piece = slice(i * 48, (i + 1) * 48)
        alive = own_live[piece]
        rows = handed[piece, :].astype(F32) + (branch[piece] + down_bias[...])
        rows = jnp.where(alive, rows, 0.0).astype(BF16)
        result[0, 0, piece, :] = rows[:, :HD]
        result[0, 1, piece, :] = rows[:, HD:]
    hand_out(0)

    stat[0] = jnp.zeros((H, 128), F32)
    stat[1] = jnp.zeros((H, 128), F32)

    @pl.loop(0, NT)
    def _(tile):
        at = pl.ds(aligned(tile * T, T), T)
        grad = dot_t(up[...], wd[at, :])
        total_gain = jnp.zeros((8, T), F32)
        total_bias = jnp.zeros((8, T), F32)
        for i in range(9):
            piece = slice(i * 32, (i + 1) * 32)
            g = grad[piece]
            vhat = vh[piece, at].astype(F32)
            tmp[piece, at] = g
            gv = g * vhat
            total_gain += by8(gv)
            total_bias += by8(g)
            gain = fourth_gain[:, at]
            g, gv = g * gain, gv * gain
            stat[0, piece, :] += g[:, :128] + g[:, 128:]
            stat[1, piece, :] += gv[:, :128] + gv[:, 128:]
        cols[0, tile] = total_gain
        cols[1, tile] = total_bias

    for i in range(2):
        mean = jnp.sum(stat[i], axis=1, keepdims=True) * (1.0 / FF)
        stat[i] = jnp.broadcast_to(mean, (H, 128))
    for copy in c_fs:
        copy.wait_send()
    gi = fs

    @pl.loop(0, NT)
    def _(tile):
        at = pl.ds(aligned(tile * T, T), T)
        total = jnp.zeros((8, T), F32)
        for i in range(9):
            piece = slice(i * 32, (i + 1) * 32)
            m1, m2, s = stat[0, piece, :], stat[1, piece, :], stat[2, piece, :]
            vhat = vh[piece, at].astype(F32)
            grad = tmp[piece, at] * fourth_gain[:, at] - jnp.concatenate([m1, m1], 1)
            grad = (grad - vhat * jnp.concatenate([m2, m2], 1)) * jnp.concatenate([s, s], 1)
            low = (grad * dg[piece, at].astype(F32)).astype(BF16)
            gi[piece, at] = low
            total += by8(low.astype(F32))
        cols[2, tile] = total

    c_gi = cp.go(gi.at[:, pl.ds(aligned((1 - c) * (FF // 2), 128), FF // 2)], gi_sib, sib)
    gfn[...] = dot_t(gi[...], wi[...])

    total_gain = jnp.zeros((8, D), F32)
    total_bias = jnp.zeros((8, D), F32)
    total_out = jnp.zeros((8, D), F32)
    for i in range(6):
        piece = slice(i * 48, (i + 1) * 48)
        vhat, scale = normal(handed[piece, :].astype(F32))
        grad = gfn[piece, :]
        total_gain += by8(grad * vhat)
        total_bias += by8(grad)
        low = (
            up[piece, :].astype(F32) + normal_back(vhat, scale, third_gain[...], grad)
        ).astype(BF16)
        hgr[piece, :] = low
        total_out += by8(low.astype(F32))

    def store_vector(row, total):
        bv[row : row + 1, :] = jnp.sum(total, axis=0, keepdims=True)

    store_vector(6, total_out)
    store_vector(7, total_gain)
    store_vector(8, total_bias)
    c_hg = cp.go(hgr.at[:, pl.ds(aligned((1 - c) * HD, 128), HD)], hg_sib, sib)

    gfn[...] = dot_t(hgr[...], wo[...])
    total_gain = jnp.zeros((8, D), F32)
    total_bias = jnp.zeros((8, D), F32)
    for i in range(6):
        piece = slice(i * 48, (i + 1) * 48)
        vhat, scale = normal(mixed[piece, :])
        grad = gfn[piece, :]
        total_gain += by8(grad * vhat)
        total_bias += by8(grad)
        gmix[piece, :] = normal_back(vhat, scale, second_gain[...], grad).astype(BF16)
    store_vector(4, total_gain)
    store_vector(5, total_bias)
    c_gmix = cp.go(
        gmix.at[:, pl.ds(aligned((1 - c) * HD, 128), HD)], do.at[pl.ds(own, H)], sib
    )
    do[pl.ds(own, H), :] = gmix[:, pl.ds(heads_at, HD)]

    c_fn.wait_recv()
    c_gi.wait_recv()

    def fn_rows(at):
        return lambda i, h: fn[pl.ds(at, H), h * HD : (h + 1) * HD]

    units(
        4, 4, fn_rows(own), fn_rows(other),
        lambda i: jnp.concatenate(
            [gi[:, pl.ds(aligned(c * (FF // 2) + i * HD, 128), HD)], gi_sib[:, i * HD : (i + 1) * HD]], 0
        ),
    )
    c_sub.wait_recv()
    c_hg.wait_recv()

    def sub_rows(at):
        return lambda i, h: sub[pl.ds(at, H), h * HD : (h + 1) * HD]

    units(
        8, 1, sub_rows(own), sub_rows(other),
        lambda i: jnp.concatenate([hgr[:, pl.ds(heads_at, HD)], hg_sib[...]], 0),
    )

    c_gmix.wait_recv()
    for pr in range(PAIRS):
        lanes = slice(pr * 128, (pr + 1) * 128)
        for j, nk, at in reversed(blocks):
            qs = slice(j * 128, (j + 1) * 128)
            probs = pt[pr, at : at + nk, :]
            do_split = split_pair(do[qs, lanes])
            grad_probs = dot_t(v[:nk, lanes], do_split)
            exact = probs.astype(F32)
            inner_sum = jnp.sum(exact * grad_probs, axis=0, keepdims=True)
            grad_scores = (exact * (grad_probs - inner_sum)).astype(BF16)
            value_part = dot(probs, do_split)
            key_part = dot(grad_scores, split_pair(q[qs, lanes]))
            if j == len(blocks) - 1:
                gfn[:, :128] = value_part[:H]
                gfn[:, 128:256] = value_part[H:]
                gfn[:, 256:384] = key_part[:H]
                gfn[:, 384:512] = key_part[H:]
            else:
                for lane_at, part in ((0, value_part), (256, key_part)):
                    top = min(nk, H)
                    gfn[:top, lane_at : lane_at + 128] += part[:top]
                    if nk > H:
                        gfn[: nk - H, lane_at + 128 : lane_at + 256] += part[H:]
            out = dot(kt[lanes, :nk], grad_scores)
            query_part = jnp.concatenate([out[:64, :128], out[64:, 128:]], 0).T * 0.125
            count = min(128, R - j * 128)
            dqkv[j * 128 : j * 128 + count, lanes] = query_part[:count].astype(BF16)
        for half in range(2):
            rows = slice(half * H, (half + 1) * H)
            dqkv[rows, 2 * HD + pr * 128 : 2 * HD + (pr + 1) * 128] = gfn[
                :, half * 128 : (half + 1) * 128
            ].astype(BF16)
            dqkv[rows, HD + pr * 128 : HD + (pr + 1) * 128] = gfn[
                :, 256 + half * 128 : 256 + (half + 1) * 128
            ].astype(BF16)

    for i in range(3):
        for h in range(2):
            grads[9 + i, h] = t_dot(
                normed[:, h * HD : (h + 1) * HD], dqkv[:, i * HD : (i + 1) * HD]
            ).astype(BF16)
        send_unit(9 + i)
    bv[2:4, :] = jnp.zeros((2, D), F32)
    for row, at in ((2, 0), (3, 2 * HD)):
        total = jnp.zeros((8, HD), F32)
        for i in range(12):
            total += by8(dqkv[i * 48 : (i + 1) * 48, at : at + HD].astype(F32))
        bv[row : row + 1, pl.ds(heads_at, HD)] = jnp.sum(total, axis=0, keepdims=True)

    for part, at in ((0, other), (1, own)):
        total = jnp.zeros((H, D), F32)
        for i in range(3):
            total += dot_t(dqkv[pl.ds(at, H), i * HD : (i + 1) * HD], wj[i])
        tmp[:, part * D : (part + 1) * D] = total
        if part == 0:
            c_gn = cp.go(tmp.at[:, :D], gn_sib, sib)
    c_gn.wait_recv()
    total_gain = jnp.zeros((8, D), F32)
    total_bias = jnp.zeros((8, D), F32)
    total_down = jnp.zeros((8, D), F32)
    for i in range(6):
        piece = slice(i * 48, (i + 1) * 48)
        vhat, scale = normal(feature_rows(own + i * 48, 48))
        grad = tmp[piece, D : 2 * D] + gn_sib[piece, :]
        total_gain += by8(grad * vhat)
        total_bias += by8(grad)
        total_down += by8(up[piece, :].astype(F32))
        rows = (
            hgr[piece, :].astype(F32) + normal_back(vhat, scale, first_gain[...], grad)
        ).astype(BF16)
        result[1, 0, piece, :] = rows[:, :HD]
        result[1, 1, piece, :] = rows[:, HD:]
    hand_out(1)
    store_vector(0, total_gain)
    store_vector(1, total_bias)
    store_vector(9, total_down)
    for kind, row in ((2, 10), (0, 14), (1, 18)):
        for tile in range(NT):
            bv[row + tile // 3 : row + tile // 3 + 1, (tile % 3) * T : (tile % 3 + 1) * T] = jnp.sum(
                cols[kind, tile], axis=0, keepdims=True
            )
    bv[22:24, :] = jnp.zeros((2, D), F32)

    def vector_step(i):
        if i > 0:
            copies["v", i - 1].wait_recv()
            copies["v", i - 1].wait_send()
            if i <= 3:
                bv[...] += bv_in[i - 1]
            elif i < 6:
                vector_total[0] = vector_total[0] + bv_in[i - 1]
            else:
                bv[...] = vector_total[0] + bv_in[i - 1]
                copies["v", "out"] = local(bv, bv_out)
                return
        if i == 3:
            vector_total.append(bv[...])
        source = bv if i <= 3 else bv_in.at[i - 1]
        copies["v", i] = cp.go(source, bv_in.at[i], (sib, xp, yp, nxt, nxt, nxt)[i])

    vector_total = []
    queues = {u: steps_of(u) for u in range(UNITS)}
    queues["v"] = [functools.partial(vector_step, i) for i in range(7)]
    for tick in range(60):
        for u in range(UNITS):
            if tick >= u and queues[u]:
                queues[u].pop(0)()
        if tick >= 4 and queues["v"]:
            queues["v"].pop(0)()

    @pl.when(home)
    def _():
        for copy in c_native + [c_ends] + c_pass:
            copy.wait_send()

    @pl.when(away)
    def _():
        for copy in c_cross + [cot_cross]:
            copy.wait_send()

    handed_out(0)
    handed_out(1)
    for copy, here in deliveries:
        copy.wait_recv()
        here.wait()
    copies["v", "out"].wait()
    done = [copies["v", i] for i in range(6)] + c_fs
    for copy in cp.open:
        if not any(copy is other for other in done):
            copy.wait_send()


def finish_kernel(gj, go, gi, gd, bv, oj, oo, oi, od, *vectors):
    oj[...] = gj[...].astype(F32)
    oo[...] = go[...].astype(F32)
    oi[...] = gi[...].astype(F32)
    od[...] = gd[...].astype(F32)

    @pl.when(pl.program_id(0) == 0)
    def _():
        x = lax.axis_index("section")
        HD = oo.shape[1] // 2
        at = pl.ds(aligned(x * HD, 128), HD)
        for row in range(10):
            vectors[row][...] = bv[row : row + 1, at]
        for i in range(3):
            row = 10 + 4 * i
            for j in range(2):
                low, high = bv[row + j : row + j + 1, :], bv[row + 2 + j : row + 3 + j, :]
                vectors[10 + i][:, 2 * j * HD : 2 * (j + 1) * HD] = jnp.where(x == 0, low, high)


def per_device(
    inputs, seq_lengths, cotangent,
    first_gain, first_bias, joint_weight, query_bias, value_bias, second_gain, second_bias,
    output_weight, output_bias, third_gain, third_bias, inner_weight, inner_bias,
    fourth_gain, fourth_bias, down_weight, down_bias,
):
    R, HD = inputs.shape
    D, H, FF = 2 * HD, R // 2, inner_weight.shape[1]
    hbm = pl.BlockSpec(memory_space=pl.ANY)
    vmem = pl.BlockSpec(memory_space=pltpu.VMEM)
    flat = [
        m.reshape(1, -1)
        for m in (
            first_gain, first_bias, query_bias, value_bias, second_gain, second_bias, output_bias,
            third_gain, third_bias, inner_bias, fourth_gain, fourth_bias, down_bias,
        )
    ]
    V = pltpu.VMEM
    scratch = [
        V((3, D, HD), BF16), V((D, D), BF16), V((D, FF), BF16), V((FF, D), BF16),
        V((2, R, HD), BF16), V((2, R, HD), BF16), V((8, 128), F32), V((R, D), BF16),
        V((640, HD), BF16), V((R, HD), BF16), V((R, HD), BF16),
        V((HD, 640), BF16), V((HD, 640), BF16), V((R, 640), BF16),
        V((PAIRS, 128 * 10 + R, 256), BF16),
        V((640, HD), F32), V((H, D), F32),
        V((R, D), BF16), V((R, D), BF16), V((H, D), BF16),
        V((H, FF), F32), V((H, FF), BF16), V((H, FF), BF16),
        V((H, FF), BF16), V((H, FF // 2), BF16), V((H, FF // 2), BF16),
        V((H, D), BF16), V((H, D), F32), V((H, D), BF16), V((H, HD), BF16),
        V((H, D), BF16), V((640, HD), BF16), V((R, 3 * HD), BF16),
        V((H, D), F32), V((2, 2, H, HD), BF16), V((3, H, 128), F32),
        V((3, FF // 256, 8, 256), F32), V((24, D), F32), V((6, 24, D), F32),
        V((UNITS, 2, HD, HD), BF16), V((UNITS, HD, HD), BF16), V((UNITS, HD // 2, HD), BF16),
        V((UNITS, 3, HD // 8, HD), BF16), V((len(Y_FIRST), HD, HD), BF16),
        pltpu.SemaphoreType.DMA((32,)), pltpu.SemaphoreType.DMA((200,)), pltpu.SemaphoreType.DMA((200,)),
    ]
    shape = jax.ShapeDtypeStruct
    result, input_grad, gj, go, gi, gd, bv = pl.pallas_call(
        layer_kernel,
        out_shape=[
            shape((R, HD), BF16), shape((R, HD), BF16),
            shape((HD, 3 * D), BF16), shape((HD, D), BF16), shape((HD, FF), BF16),
            shape((FF // 2, D), BF16), shape((24, D), F32),
        ],
        in_specs=[hbm, hbm, vmem, hbm, hbm, hbm, hbm] + [vmem] * 13,
        out_specs=[hbm] * 7,
        scratch_shapes=scratch,
        compiler_params=pltpu.CompilerParams(
            collective_id=0, has_side_effects=True, vmem_limit_bytes=66_000_000
        ),
        cost_estimate=pl.CostEstimate(flops=16 * 10**9, bytes_accessed=25 * 10**6, transcendentals=4 * 10**6),
    )(inputs, cotangent, seq_lengths, joint_weight, output_weight, inner_weight, down_weight, *flat)
    steps = 8
    wide = [(HD, 3 * D), (HD, D), (HD, FF), (FF // 2, D)]

    def block(rows, columns):
        return pl.BlockSpec((rows // steps, columns), lambda i: (i, 0))

    def fixed(rows, columns):
        return pl.BlockSpec((rows, columns), lambda i: (0, 0))

    small = [(1, HD)] * 10 + [(1, FF // 2)] * 3
    groups = lax.axis_size("batch") // GROUP
    if groups > 1:
        peers = [[r + GROUP * g for g in range(groups)] for r in range(GROUP)]
        gj, go, gi, gd, bv = lax.psum(
            tuple(m.astype(F32) for m in (gj, go, gi, gd, bv)), "batch", axis_index_groups=peers
        )
    outs = pl.pallas_call(
        finish_kernel,
        grid=(steps,),
        out_shape=[shape(s, F32) for s in wide + small],
        in_specs=[block(*s) for s in wide] + [fixed(24, D)],
        out_specs=[block(*s) for s in wide] + [fixed(*s) for s in small],
        compiler_params=pltpu.CompilerParams(vmem_limit_bytes=48 * 2**20),
    )(gj, go, gi, gd, bv)
    dj, dout, di, dd = outs[:4]
    vec = [m.reshape(-1) for m in outs[4:]]
    fg, fb, qb, vb, sg, sb, ob, tg, tb, db, ib, hg, hb = vec
    return (
        result, input_grad, fg, fb, dj, qb, vb, sg, sb, dout, ob, tg, tb, di, ib, hg, hb, dd, db,
    )


def solution(mesh):
    wide = P("section", None)
    line = P("section")
    return jax.shard_map(
        per_device,
        mesh=mesh,
        in_specs=(P("batch", "section"), P("batch", None), P("batch", "section")) + (P(),) * 17,
        out_specs=(
            P("batch", "section"), P("batch", "section"), line, line, wide, line, line, line, line,
            wide, line, line, line, wide, line, line, line, wide, line,
        ),
        check_vma=False,
    )
```

profile of v0, /device:TPU:1, one launch (start us, length us, event | category | flops | bytes accessed | tf_op | source)
XLA Modules:
  0.0 231.5 jit_solution(16696839957980696211)
XLA Ops:
  0.7 1.3 reshape.116.first_gain
  1.9 1.3 reshape.117.first_bias
  3.2 1.3 reshape.118.query_bias
  4.5 1.3 reshape.119.value_bias
  5.7 1.3 reshape.120.second_gain
  7.0 1.3 reshape.121.second_bias
  8.3 1.3 reshape.122.output_bias
  9.5 1.3 reshape.123.third_gain
  10.8 1.3 reshape.124.third_bias
  12.1 1.3 reshape.128.down_bias
  13.3 195.9 %shard_map.339 = (bf16[576,384]{1,0:T(8,128)(2,1)}, bf16[576,384]{1,0:T(8,128)(2,1)}, bf16[384,2304]{1,0:T(8,128)(2,1)}, bf16[384,768]{1,0:T(8,128)(2,1)}, bf16[...) custom-call(bf16[576,384]{1,0:T(8,128)(2,1)} %x_in.1, bf16[576,384]{1,0:T(8,128)(2,1)} %cot_in.1, ...), custom_call_target="tpu_custom_call" | custom-call | flops 16000000000 | bytes 25000000 | tf_op jit(solution)/shard_map/pallas_call | solution.py:849
  209.2 1.7 copy-done
  210.9 1.5 copy-done.1
  212.4 1.1 copy-done.2
  213.4 0.9 copy-done.3
  214.3 7.9 %shard_map.340 = (f32[384,2304]{1,0:T(8,128)}, f32[384,768]{1,0:T(8,128)}, f32[384,3072]{1,0:T(8,128)}, f32[1536,768]{1,0:T(8,128)}, f32[1,384]{1,0:T(1,128)S(1)...) custom-call(bf16[384,2304]{1,0:T(8,128)(2,1)S(1)} %copy-done.1, ...), custom_call_target="tpu_custom_call" | custom-call | tf_op jit(solution)/shard_map/pallas_call | solution.py:880
  222.8 0.6 reduce.1
  224.0 0.6 reduce.3
  225.1 0.6 reduce.5
  228.1 0.6 reduce.9
  228.7 0.6 reduce.10
  229.4 0.6 reduce.11
  230.0 0.8 copy.41
  230.7 0.8 copy.42
  (15 shorter events, 4.2 us)
Async XLA Ops:
  209.2 1.7 copy-start
  210.9 1.5 copy-start.1
  212.4 1.1 copy-start.2
  213.4 0.9 copy-start.3
  214.3 15.7 %copy-start.5 = (bf16[576,384]{1,0:T(8,128)(2,1)S(1)}, bf16[576,384]{1,0:T(8,128)(2,1)}, u32[]{:S(2)}) copy-start(bf16[576,384]{1,0:T(8,128)(2,1)} %get-tuple-element.86) | copy-start | bytes 1327108
  214.3 16.4 %copy-start.4 = (bf16[576,384]{1,0:T(8,128)(2,1)S(1)}, bf16[576,384]{1,0:T(8,128)(2,1)}, u32[]{:S(2)}) copy-start(bf16[576,384]{1,0:T(8,128)(2,1)} %get-tuple-element.87) | copy-start | bytes 1327108
where the time goes:
time: 232 us
  Pallas kernels  204 us (88%)
  local copies, waits for them, and re-layouts  19.3 us (8%)
  other arithmetic  7.81 us (3%)
    pallas_call x1, Pallas kernels, per_device(): pl.pallas_call(layer_kernel, out_shape=[shape((R, HD), BF16), shape((R, H...  196 us
    reshape x10, local copies, waits for them, and re-layouts, per_device(): m.reshape(1, -1)  12.7 us
    pallas_call x1, Pallas kernels, per_device(): pl.pallas_call(finish_kernel, grid=(steps,), out_shape=[shape(s, F32) for...  7.86 us
    pallas_call x13, other arithmetic, per_device(): pl.pallas_call(finish_kernel, grid=(steps,), out_shape=[shape(s, F32) for...  7.81 us
    unnamed x14, local copies, waits for them, and re-layouts  6.61 us

commit v1 on v0

--- a/solution.py
+++ b/solution.py
@@ -16,14 +16,39 @@
 GROUP = 16
 PAIRS = HEADS // 4
 UNITS = 12
-Y_FIRST = (1, 4, 7, 10)
-Y_GATHER = (1, 3, 5, 7, 9, 11)
+AXES = ("x", "y", "a", "b")
+SUM_ORDER = ("axyb", "xyab", "yaxb", "aybx", "abxy", "yaxb", "xayb", "xyab", "yxab", "xyab", "yxab", "yxab")
+GATHER_ORDER = ("bay", "bay", "bay", "bay", "bya", "bay", "bay", "bay", "bya", "bay", "bya", "bay")
+SCHEDULE = (
+    (0, ((0, 0),)),
+    (1, ((1, 0),)),
+    (2, ((2, 0),)),
+    (3, ()),
+    ("result", ((3, 0),)),
+    ("down_back0", ()),
+    ("down_back1", ((0, 1), (1, 1))),
+    ("down_back2", ((2, 1),)),
+    ("inner_back0", ()),
+    ("inner_back1", ()),
+    ("gfn", ()),
+    ("handed", ((1, 2), (3, 1))),
+    ("mixed", ()),
+    (4, ((4, 0), (0, 2))),
+    (5, ((2, 2), (5, 0))),
+    (6, ((6, 0),)),
+    (7, ((1, 3), (3, 2))),
+    (8, ()),
+    ("heads0", ((0, 3), (2, 3))),
+    ("heads1", ((7, 0), (8, 0))),
+    ("heads2", ((4, 1), (5, 1), (6, 1), (1, 4))),
+    (9, ((3, 3),)),
+    (10, ((0, 4), (10, 0))),
+    (11, ((2, 4), (9, 0))),
+    ("joint_back", ()),
+    ("end", ((8, 1), ("v", 0), (7, 1), (3, 4), ("v", 1), (5, 2), (4, 2), (11, 0), (6, 2), (10, 1), (1, 5), (9, 1), (0, 5), (2, 5), (3, 5), (7, 2), (1, 6), (0, 6), (2, 6), (3, 6), (8, 2), (11, 1), (7, 3), ("v", 2), (6, 3), (5, 3), (8, 3), (4, 3), (7, 4), (9, 2), (6, 4), (10, 2), (5, 4), (1, 7), (9, 3), (8, 4), (11, 2), (7, 5), (10, 3), (0, 7), (6, 5), (5, 5), (2, 7), (11, 3), (9, 4), (7, 6), (8, 5), (3, 7), (10, 4), (6, 6), ("v", 3), (4, 4), (5, 6), (11, 4), (9, 5), (7, 7), (10, 5), ("v", 4), (8, 6), (4, 5), (11, 5), (9, 6), (6, 7), ("v", 5), (5, 7), (8, 7), (10, 6), (11, 6), (4, 6), (9, 7), (10, 7), (11, 7), (4, 7))),
+)
 GELU_C = 0.7978845608028654
 GELU_A = 0.044715
-
-
-def gray(v):
-    return v + (v // 2) * (1 - 2 * (v % 2))
 
 
 def aligned(v, by):
@@ -78,27 +103,91 @@
             device_id_type=MESH,
         )
 
-    def go(self, src, dst, device):
+    def go(self, src, dst, device, keep=True):
         copy = self.remote(src, dst, device)
         copy.start()
-        self.open.append(copy)
+        if keep:
+            self.open.append(copy)
         return copy
 
     def drain(self):
         for copy in self.open:
             copy.wait_send()
-        self.open = []
+
+
+class Sums:
+    def __init__(self, cp, here, peers, grads, parts, whole, bv, bv_in, deliver):
+        self.cp, self.here, self.peers, self.deliver = cp, here, peers, deliver
+        self.grads, self.parts, self.whole = grads, parts, whole
+        self.bv, self.bv_in, self.copies = bv, bv_in, {}
+
+    def send_part(self, u, k):
+        order = SUM_ORDER[u]
+        fixed = {axis: self.here[axis] for axis in order[:k]}
+        fixed[order[k]] = 1 - self.here[order[k]]
+        at = (u,) + tuple(fixed.get(axis, slice(None)) for axis in AXES)
+        self.copies[u] = self.cp.go(self.grads.at[at], self.parts[k].at[u], self.peers[order[k]])
+
+    def add_part(self, u, k, **side):
+        fixed = {axis: self.here[axis] for axis in SUM_ORDER[u][: k + 1]}
+        free = [axis for axis in AXES if axis not in fixed]
+        at = (u,) + tuple({**side, **fixed}.get(axis, slice(None)) for axis in AXES)
+        part = (u,) + tuple(side.get(axis, slice(None)) for axis in free)
+        total = self.grads[at].astype(F32) + self.parts[k][part].astype(F32)
+        return at, total.astype(BF16)
+
+    def send_gather(self, u, k):
+        order = GATHER_ORDER[u]
+        at = (u,) + tuple(
+            self.here[axis] if axis in order[k:] else slice(None) for axis in AXES[1:]
+        )
+        self.copies[u] = self.cp.go(self.whole.at[at], self.whole.at[at], self.peers[order[k]])
+
+    def step(self, u, i):
+        if u == "v":
+            self.vector(i)
+            return
+        if i > 0:
+            self.copies[u].wait_recv()
+        if i == 0:
+            self.send_part(u, 0)
+        elif i < 4:
+            axis = SUM_ORDER[u][i]
+            at, total = self.add_part(u, i - 1, **{axis: 1 - self.here[axis]})
+            self.grads[at] = total
+            self.send_part(u, i)
+            at, total = self.add_part(u, i - 1, **{axis: self.here[axis]})
+            self.grads[at] = total
+        elif i == 4:
+            at, total = self.add_part(u, 3)
+            self.whole[(u,) + at[2:]] = total
+            self.send_gather(u, 0)
+        elif i < 7:
+            self.send_gather(u, i - 4)
+        else:
+            self.deliver(u, self.whole.at[u])
+
+    def vector(self, i):
+        if i > 0:
+            self.copies["v"].wait_recv()
+            self.copies["v"].wait_send()
+            self.bv[...] += self.bv_in[i - 1]
+        if i < 5:
+            to = self.peers[("c", *AXES)[i]]
+            self.copies["v"] = self.cp.go(self.bv, self.bv_in.at[i], to, keep=False)
+        else:
+            self.deliver("v", self.bv)
 
 
 def layer_kernel(
     x_in, cot_in, lens, wj_in, wo_in, wi_in, wd_in,
     first_gain, first_bias, query_bias, value_bias, second_gain, second_bias, output_bias,
-    third_gain, third_bias, inner_bias, fourth_gain, fourth_bias, down_bias,
+    third_gain, third_bias, down_bias, inner_bias, fourth_gain, fourth_bias,
     res_out, grad_out, gj_out, go_out, gi_out, gd_out, bv_out,
     wj, wo, wi, wd, feats, cots, ends, normed, q, k, v, vt, kt, bias, pt, mixed_own, mixed,
     sub, fn, handed, tmp, vh, dg, fs, fs_sib, gi_sib, up, gfn, hgr, hg_sib, gmix, do, dqkv,
-    gn_sib, result, stat, cols, bv, bv_in, grads, r1, r2, rz, oy,
-    lsem, ssem, rsem,
+    result, stat, cols, bv, bv_in, grads, r1, r2, r3, r4, whole,
+    vectors, lsem, ssem, rsem,
 ):
     R, HD = x_in.shape
     D = 2 * HD
@@ -110,7 +199,7 @@
     b = lax.axis_index("batch")
     base = (b // GROUP) * GROUP
     z, y, c = (b // 4) % 4, (b // 2) % 2, b % 2
-    p = gray(z)
+    low, high = z % 2, z // 2
 
     def dev(x_, z_, y_, c_):
         return (x_, base + z_ * 4 + y_ * 2 + c_)
@@ -119,8 +208,10 @@
     xp = dev(1 - x, z, y, c)
     xc = dev(1 - x, z, y, 1 - c)
     yp = dev(x, z, 1 - y, c)
-    nxt = dev(x, gray((p + 1) % 4), y, c)
-    prv = dev(x, gray((p + 3) % 4), y, c)
+    peers = {
+        "c": sib, "x": xp, "y": yp,
+        "a": dev(x, 2 * high + 1 - low, y, c), "b": dev(x, 2 * (1 - high) + low, y, c),
+    }
     home = c == x
     away = c != x
     own = aligned(c * H, 32)
@@ -139,8 +230,19 @@
     wi_copy = local(wi_in, wi)
     wd_copy = local(wd_in, wd)
 
+    lines = (
+        first_gain, first_bias, query_bias, value_bias, second_gain, second_bias, output_bias,
+        third_gain, third_bias, down_bias,
+    )
+    for i, line in enumerate(lines):
+        vectors[i : i + 1, :] = line[...].reshape(1, D)
+    (
+        first_gain, first_bias, query_bias, value_bias, second_gain, second_bias, output_bias,
+        third_gain, third_bias, down_bias,
+    ) = (vectors.at[i : i + 1] for i in range(len(lines)))
+
     barrier = pltpu.get_barrier_semaphore()
-    for peer in (sib, xp, xc, yp, nxt, prv):
+    for peer in (*peers.values(), xc):
         pl.semaphore_signal(barrier, inc=1, device_id=peer, device_id_type=MESH)
     pl.semaphore_wait(barrier, 6)
 
@@ -335,6 +437,7 @@
             fs.at[:, pl.ds(aligned((2 * i + 1 - c) * D, 128), D)],
             fs_sib.at[:, i * D : (i + 1) * D],
             sib,
+            keep=False,
         )
         for i in range(2)
     ]
@@ -362,129 +465,43 @@
     up[:, :HD] = cots[0, pl.ds(own, H), :]
     up[:, HD:] = cots[1, pl.ds(own, H), :]
 
-    events = []
+    deliveries = []
+
+    def deliver(u, total):
+        if u == "v":
+            deliveries.append((None, local(total, bv_out)))
+            return
+        rows = (slice(None),) * 4
+        if u < 4:
+            target = gd_out.at[(c, u // 2) + rows + (slice((u % 2) * HD, (u % 2 + 1) * HD),)]
+        elif u < 8:
+            target = gi_out.at[rows + (pl.ds(aligned(c * (FF // 2) + (u - 4) * HD, 128), HD),)]
+        elif u == 8:
+            target = go_out.at[rows + (pl.ds(heads_at, HD),)]
+        else:
+            target = gj_out.at[rows + (pl.ds(aligned((u - 9) * D + c * HD, 128), HD),)]
+        deliveries.append((cp.go(total, target, sib), local(total, target)))
+
+    here = {"x": x, "y": y, "a": low, "b": high}
+    sums = Sums(cp, here, peers, grads, (r1, r2, r3, r4), whole, bv, bv_in, deliver)
+    schedule = iter(SCHEDULE)
+
+    def pump(mark):
+        at, steps = next(schedule)
+        assert at == mark
+        for u, i in steps:
+            sums.step(u, i)
+
+
+    def cut_rows(unit):
+        return unit.astype(BF16).reshape(2, 2, 2, HD // 8, HD)
 
     def units(first, count, left_own, left_sib, right):
         for i in range(count):
             for h in range(2):
                 rows = jnp.concatenate([left_own(i, h), left_sib(i, h)], 0)
-                grads[first + i, h] = t_dot(rows, right(i)).astype(BF16)
-            send_unit(first + i)
-
-    copies = {}
-    half_rows = HD // 2
-    piece_rows = HD // 8
-
-    def y_rows(y_):
-        return pl.ds(aligned(y_ * half_rows, 32), half_rows)
-
-    def z_rows(piece, y_=None):
-        y_ = y if y_ is None else y_
-        return pl.ds(aligned(y_ * half_rows + piece * piece_rows, 16), piece_rows)
-
-    def add(dst, rows, src, src_rows):
-        dst[rows, :] = (dst[rows, :].astype(F32) + src[src_rows, :].astype(F32)).astype(BF16)
-
-    def send_unit(u):
-        if u in Y_FIRST:
-            for h in range(2):
-                copies[u, "a", h] = cp.go(
-                    grads.at[u, h, y_rows(1 - y)], r1.at[u, h * half_rows : (h + 1) * half_rows], yp
-                )
-        else:
-            copies[u, "a"] = cp.go(grads.at[u, 1 - x], r1.at[u], xp)
-
-    def second(u):
-        mine = grads.at[u, x]
-        if u in Y_FIRST:
-            for h in range(2):
-                copies[u, "a", h].wait_recv()
-            theirs = grads.at[u, 1 - x]
-            add(theirs, y_rows(y), r1.at[u], y_rows(1 - x))
-            copies[u, "b"] = cp.go(theirs.at[y_rows(y)], r2.at[u], xp)
-            add(mine, y_rows(y), r1.at[u], y_rows(x))
-        else:
-            copies[u, "a"].wait_recv()
-            add(mine, y_rows(1 - y), r1.at[u], y_rows(1 - y))
-            copies[u, "b"] = cp.go(mine.at[y_rows(1 - y)], r2.at[u], yp)
-            add(mine, y_rows(y), r1.at[u], y_rows(y))
-
-    def third(u):
-        mine = grads.at[u, x]
-        copies[u, "b"].wait_recv()
-        for s in range(4):
-            piece = (p + 3 - s) % 4
-            add(mine, z_rows(piece), r2.at[u], pl.ds(aligned(piece * piece_rows, 16), piece_rows))
-            if s == 0:
-                copies[u, "z", 0] = cp.go(mine.at[z_rows(piece)], rz.at[u, 0], nxt)
-
-    def whole(u):
-        return oy.at[Y_FIRST.index(u)] if u in Y_FIRST else r1.at[u]
-
-    def ring(u, s):
-        mine = grads.at[u, x]
-        copies[u, "z", s].wait_recv()
-        piece = (p + 2 - s) % 4
-        if s < 2:
-            add(mine, z_rows(piece), rz.at[u, s], pl.ds(0, piece_rows))
-            copies[u, "z", s + 1] = cp.go(mine.at[z_rows(piece)], rz.at[u, s + 1], nxt)
-        else:
-            out = whole(u)
-            out[z_rows(p), :] = (
-                mine[z_rows(p), :].astype(F32) + rz[u, 2].astype(F32)
-            ).astype(BF16)
-            if u in Y_GATHER:
-                copies[u, "gy"] = cp.go(out.at[z_rows(p)], out.at[z_rows(p)], yp)
-            else:
-                copies[u, "gz", 0] = [cp.go(out.at[z_rows(p)], out.at[z_rows(p)], nxt)]
-
-    def gather_z(u, s):
-        out = whole(u)
-        for copy in copies[u, "gz", s]:
-            copy.wait_recv()
-        piece = (p + 3 - s) % 4
-        sides = (0, 1) if u in Y_GATHER else (y,)
-        if s < 2:
-            copies[u, "gz", s + 1] = [
-                cp.go(out.at[z_rows(piece, side)], out.at[z_rows(piece, side)], nxt)
-                for side in sides
-            ]
-        elif u in Y_GATHER:
-            deliver(u)
-        else:
-            copies[u, "gy"] = cp.go(out.at[y_rows(y)], out.at[y_rows(y)], yp)
-
-    def gather_y(u):
-        copies[u, "gy"].wait_recv()
-        out = whole(u)
-        if u in Y_GATHER:
-            copies[u, "gz", 0] = [
-                cp.go(out.at[z_rows(p, side)], out.at[z_rows(p, side)], nxt) for side in (0, 1)
-            ]
-        else:
-            deliver(u)
-
-    deliveries = []
-
-    def deliver(u):
-        if u < 4:
-            target = gd_out.at[pl.ds(aligned(c * D + (u // 2) * HD, 128), HD), (u % 2) * HD : (u % 2 + 1) * HD]
-        elif u < 8:
-            target = gi_out.at[:, pl.ds(aligned(c * (FF // 2) + (u - 4) * HD, 128), HD)]
-        elif u == 8:
-            target = go_out.at[:, pl.ds(heads_at, HD)]
-        else:
-            target = gj_out.at[:, pl.ds(aligned((u - 9) * D + c * HD, 128), HD)]
-        copy = cp.go(whole(u), target, sib)
-        deliveries.append((copy, local(whole(u), target)))
-
-    def steps_of(u):
-        steps = [functools.partial(second, u), functools.partial(third, u)]
-        steps += [functools.partial(ring, u, s) for s in range(3)]
-        gather = [functools.partial(gather_z, u, s) for s in range(3)]
-        if u in Y_GATHER:
-            return steps + [functools.partial(gather_y, u)] + gather
-        return steps + gather + [functools.partial(gather_y, u)]
+                grads[first + i, h] = cut_rows(t_dot(rows, right(i)))
+            pump(first + i)
 
     for copy in c_fs:
         copy.wait_recv()
@@ -543,12 +560,12 @@
         result[0, 0, piece, :] = rows[:, :HD]
         result[0, 1, piece, :] = rows[:, HD:]
     hand_out(0)
+    pump("result")
 
     stat[0] = jnp.zeros((H, 128), F32)
     stat[1] = jnp.zeros((H, 128), F32)
 
-    @pl.loop(0, NT)
-    def _(tile):
+    def down_back(tile):
         at = pl.ds(aligned(tile * T, T), T)
         grad = dot_t(up[...], wd[at, :])
         total_gain = jnp.zeros((8, T), F32)
@@ -568,6 +585,10 @@
         cols[0, tile] = total_gain
         cols[1, tile] = total_bias
 
+    for i in range(3):
+        pl.loop(i * NT // 3, (i + 1) * NT // 3)(down_back)
+        pump(f"down_back{i}")
+
     for i in range(2):
         mean = jnp.sum(stat[i], axis=1, keepdims=True) * (1.0 / FF)
         stat[i] = jnp.broadcast_to(mean, (H, 128))
@@ -575,8 +596,7 @@
         copy.wait_send()
     gi = fs
 
-    @pl.loop(0, NT)
-    def _(tile):
+    def inner_back(tile):
         at = pl.ds(aligned(tile * T, T), T)
         total = jnp.zeros((8, T), F32)
         for i in range(9):
@@ -590,8 +610,13 @@
             total += by8(low.astype(F32))
         cols[2, tile] = total
 
+    for i in range(2):
+        pl.loop(i * NT // 2, (i + 1) * NT // 2)(inner_back)
+        pump(f"inner_back{i}")
+
     c_gi = cp.go(gi.at[:, pl.ds(aligned((1 - c) * (FF // 2), 128), FF // 2)], gi_sib, sib)
     gfn[...] = dot_t(gi[...], wi[...])
+    pump("gfn")
 
     total_gain = jnp.zeros((8, D), F32)
     total_bias = jnp.zeros((8, D), F32)
@@ -615,6 +640,8 @@
     store_vector(7, total_gain)
     store_vector(8, total_bias)
     c_hg = cp.go(hgr.at[:, pl.ds(aligned((1 - c) * HD, 128), HD)], hg_sib, sib)
+
+    pump("handed")
 
     gfn[...] = dot_t(hgr[...], wo[...])
     total_gain = jnp.zeros((8, D), F32)
@@ -632,6 +659,8 @@
         gmix.at[:, pl.ds(aligned((1 - c) * HD, 128), HD)], do.at[pl.ds(own, H)], sib
     )
     do[pl.ds(own, H), :] = gmix[:, pl.ds(heads_at, HD)]
+
+    pump("mixed")
 
     c_fn.wait_recv()
     c_gi.wait_recv()
@@ -692,13 +721,14 @@
             dqkv[rows, HD + pr * 128 : HD + (pr + 1) * 128] = gfn[
                 :, 256 + half * 128 : 256 + (half + 1) * 128
             ].astype(BF16)
+        pump(f"heads{pr}")
 
     for i in range(3):
         for h in range(2):
-            grads[9 + i, h] = t_dot(
-                normed[:, h * HD : (h + 1) * HD], dqkv[:, i * HD : (i + 1) * HD]
-            ).astype(BF16)
-        send_unit(9 + i)
+            grads[9 + i, h] = cut_rows(
+                t_dot(normed[:, h * HD : (h + 1) * HD], dqkv[:, i * HD : (i + 1) * HD])
+            )
+        pump(9 + i)
     bv[2:4, :] = jnp.zeros((2, D), F32)
     for row, at in ((2, 0), (3, 2 * HD)):
         total = jnp.zeros((8, HD), F32)
@@ -712,15 +742,16 @@
             total += dot_t(dqkv[pl.ds(at, H), i * HD : (i + 1) * HD], wj[i])
         tmp[:, part * D : (part + 1) * D] = total
         if part == 0:
-            c_gn = cp.go(tmp.at[:, :D], gn_sib, sib)
+            c_gn = cp.go(tmp.at[:, :D], mixed, sib)
     c_gn.wait_recv()
+    pump("joint_back")
     total_gain = jnp.zeros((8, D), F32)
     total_bias = jnp.zeros((8, D), F32)
     total_down = jnp.zeros((8, D), F32)
     for i in range(6):
         piece = slice(i * 48, (i + 1) * 48)
         vhat, scale = normal(feature_rows(own + i * 48, 48))
-        grad = tmp[piece, D : 2 * D] + gn_sib[piece, :]
+        grad = tmp[piece, D : 2 * D] + mixed[piece, :]
         total_gain += by8(grad * vhat)
         total_bias += by8(grad)
         total_down += by8(up[piece, :].astype(F32))
@@ -740,32 +771,7 @@
             )
     bv[22:24, :] = jnp.zeros((2, D), F32)
 
-    def vector_step(i):
-        if i > 0:
-            copies["v", i - 1].wait_recv()
-            copies["v", i - 1].wait_send()
-            if i <= 3:
-                bv[...] += bv_in[i - 1]
-            elif i < 6:
-                vector_total[0] = vector_total[0] + bv_in[i - 1]
-            else:
-                bv[...] = vector_total[0] + bv_in[i - 1]
-                copies["v", "out"] = local(bv, bv_out)
-                return
-        if i == 3:
-            vector_total.append(bv[...])
-        source = bv if i <= 3 else bv_in.at[i - 1]
-        copies["v", i] = cp.go(source, bv_in.at[i], (sib, xp, yp, nxt, nxt, nxt)[i])
-
-    vector_total = []
-    queues = {u: steps_of(u) for u in range(UNITS)}
-    queues["v"] = [functools.partial(vector_step, i) for i in range(7)]
-    for tick in range(60):
-        for u in range(UNITS):
-            if tick >= u and queues[u]:
-                queues[u].pop(0)()
-        if tick >= 4 and queues["v"]:
-            queues["v"].pop(0)()
+    pump("end")
 
     @pl.when(home)
     def _():
@@ -780,33 +786,39 @@
     handed_out(0)
     handed_out(1)
     for copy, here in deliveries:
-        copy.wait_recv()
+        if copy is not None:
+            copy.wait_recv()
         here.wait()
-    copies["v", "out"].wait()
-    done = [copies["v", i] for i in range(6)] + c_fs
-    for copy in cp.open:
-        if not any(copy is other for other in done):
-            copy.wait_send()
-
-
-def finish_kernel(gj, go, gi, gd, bv, oj, oo, oi, od, *vectors):
+    cp.drain()
+
+
+def finish_kernel(gj, go, gi, gd, bv, res, grad, oj, oo, oi, od, *rest):
+    *vectors, res_out, grad_out, sem = rest
+    copies = [pltpu.make_async_copy(res, res_out, sem.at[0]), pltpu.make_async_copy(grad, grad_out, sem.at[1])]
+
+    @pl.when(pl.program_id(0) == 0)
+    def _():
+        for copy in copies:
+            copy.start()
+        x = lax.axis_index("section")
+        HD = oo.shape[1] // 2
+        at = pl.ds(aligned(x * HD, 128), HD)
+        for row in range(10):
+            vectors[row][...] = bv[row : row + 1, at].reshape(HD)
+        for i in range(3):
+            row = 10 + 4 * i
+            halves = [jnp.concatenate([bv[j : j + 1, :], bv[j + 1 : j + 2, :]], 1) for j in (row, row + 2)]
+            vectors[10 + i][...] = jnp.where(x == 0, *halves).reshape(4 * HD)
+
     oj[...] = gj[...].astype(F32)
     oo[...] = go[...].astype(F32)
     oi[...] = gi[...].astype(F32)
     od[...] = gd[...].astype(F32)
 
-    @pl.when(pl.program_id(0) == 0)
+    @pl.when(pl.program_id(0) == pl.num_programs(0) - 1)
     def _():
-        x = lax.axis_index("section")
-        HD = oo.shape[1] // 2
-        at = pl.ds(aligned(x * HD, 128), HD)
-        for row in range(10):
-            vectors[row][...] = bv[row : row + 1, at]
-        for i in range(3):
-            row = 10 + 4 * i
-            for j in range(2):
-                low, high = bv[row + j : row + j + 1, :], bv[row + 2 + j : row + 3 + j, :]
-                vectors[10 + i][:, 2 * j * HD : 2 * (j + 1) * HD] = jnp.where(x == 0, low, high)
+        for copy in copies:
+            copy.wait()
 
 
 def per_device(
@@ -819,13 +831,11 @@
     D, H, FF = 2 * HD, R // 2, inner_weight.shape[1]
     hbm = pl.BlockSpec(memory_space=pl.ANY)
     vmem = pl.BlockSpec(memory_space=pltpu.VMEM)
-    flat = [
-        m.reshape(1, -1)
-        for m in (
-            first_gain, first_bias, query_bias, value_bias, second_gain, second_bias, output_bias,
-            third_gain, third_bias, inner_bias, fourth_gain, fourth_bias, down_bias,
-        )
-    ]
+    lines = (
+        first_gain, first_bias, query_bias, value_bias, second_gain, second_bias, output_bias,
+        third_gain, third_bias, down_bias,
+    )
+    lines += tuple(m.reshape(1, -1) for m in (inner_bias, fourth_gain, fourth_bias))
     V = pltpu.VMEM
     scratch = [
         V((3, D, HD), BF16), V((D, D), BF16), V((D, FF), BF16), V((FF, D), BF16),
@@ -839,19 +849,21 @@
         V((H, FF), BF16), V((H, FF // 2), BF16), V((H, FF // 2), BF16),
         V((H, D), BF16), V((H, D), F32), V((H, D), BF16), V((H, HD), BF16),
         V((H, D), BF16), V((640, HD), BF16), V((R, 3 * HD), BF16),
-        V((H, D), F32), V((2, 2, H, HD), BF16), V((3, H, 128), F32),
-        V((3, FF // 256, 8, 256), F32), V((24, D), F32), V((6, 24, D), F32),
-        V((UNITS, 2, HD, HD), BF16), V((UNITS, HD, HD), BF16), V((UNITS, HD // 2, HD), BF16),
-        V((UNITS, 3, HD // 8, HD), BF16), V((len(Y_FIRST), HD, HD), BF16),
-        pltpu.SemaphoreType.DMA((32,)), pltpu.SemaphoreType.DMA((200,)), pltpu.SemaphoreType.DMA((200,)),
+        V((2, 2, H, HD), BF16), V((3, H, 128), F32),
+        V((3, FF // 256, 8, 256), F32), V((24, D), F32), V((5, 24, D), F32),
+        V((UNITS, 2, 2, 2, 2, HD // 8, HD), BF16),
+        V((UNITS, 2, 2, 2, HD // 8, HD), BF16), V((UNITS, 2, 2, HD // 8, HD), BF16),
+        V((UNITS, 2, HD // 8, HD), BF16), V((UNITS, HD // 8, HD), BF16),
+        V((UNITS, 2, 2, 2, HD // 8, HD), BF16),
+        V((10, D), F32), pltpu.SemaphoreType.DMA((32,)), pltpu.SemaphoreType.DMA((200,)), pltpu.SemaphoreType.DMA((200,)),
     ]
     shape = jax.ShapeDtypeStruct
     result, input_grad, gj, go, gi, gd, bv = pl.pallas_call(
         layer_kernel,
         out_shape=[
             shape((R, HD), BF16), shape((R, HD), BF16),
-            shape((HD, 3 * D), BF16), shape((HD, D), BF16), shape((HD, FF), BF16),
-            shape((FF // 2, D), BF16), shape((24, D), F32),
+            *(shape((2, 2, 2, HD // 8, n), BF16) for n in (3 * D, D, FF)),
+            shape((2, 2, 2, 2, 2, HD // 8, D), BF16), shape((24, D), F32),
         ],
         in_specs=[hbm, hbm, vmem, hbm, hbm, hbm, hbm] + [vmem] * 13,
         out_specs=[hbm] * 7,
@@ -860,17 +872,15 @@
             collective_id=0, has_side_effects=True, vmem_limit_bytes=66_000_000
         ),
         cost_estimate=pl.CostEstimate(flops=16 * 10**9, bytes_accessed=25 * 10**6, transcendentals=4 * 10**6),
-    )(inputs, cotangent, seq_lengths, joint_weight, output_weight, inner_weight, down_weight, *flat)
+    )(inputs, cotangent, seq_lengths, joint_weight, output_weight, inner_weight, down_weight, *lines)
     steps = 8
     wide = [(HD, 3 * D), (HD, D), (HD, FF), (FF // 2, D)]
+    gj, go, gi, gd = (m.reshape(s) for m, s in zip((gj, go, gi, gd), wide))
 
     def block(rows, columns):
         return pl.BlockSpec((rows // steps, columns), lambda i: (i, 0))
 
-    def fixed(rows, columns):
-        return pl.BlockSpec((rows, columns), lambda i: (0, 0))
-
-    small = [(1, HD)] * 10 + [(1, FF // 2)] * 3
+    small = [(HD,)] * 10 + [(FF // 2,)] * 3
     groups = lax.axis_size("batch") // GROUP
     if groups > 1:
         peers = [[r + GROUP * g for g in range(groups)] for r in range(GROUP)]
@@ -880,14 +890,15 @@
     outs = pl.pallas_call(
         finish_kernel,
         grid=(steps,),
-        out_shape=[shape(s, F32) for s in wide + small],
-        in_specs=[block(*s) for s in wide] + [fixed(24, D)],
-        out_specs=[block(*s) for s in wide] + [fixed(*s) for s in small],
-        compiler_params=pltpu.CompilerParams(vmem_limit_bytes=48 * 2**20),
-    )(gj, go, gi, gd, bv)
+        out_shape=[shape(s, F32) for s in wide + small] + [shape((R, HD), BF16)] * 2,
+        in_specs=[block(*s) for s in wide] + [pl.BlockSpec((24, D), lambda i: (0, 0)), hbm, hbm],
+        out_specs=[block(*s) for s in wide] + [pl.BlockSpec(s, lambda i: (0,)) for s in small] + [hbm, hbm],
+        scratch_shapes=[pltpu.SemaphoreType.DMA((2,))],
+        compiler_params=pltpu.CompilerParams(vmem_limit_bytes=66_000_000),
+    )(gj, go, gi, gd, bv, result, input_grad)
+    result, input_grad = outs[-2:]
     dj, dout, di, dd = outs[:4]
-    vec = [m.reshape(-1) for m in outs[4:]]
-    fg, fb, qb, vb, sg, sb, ob, tg, tb, db, ib, hg, hb = vec
+    fg, fb, qb, vb, sg, sb, ob, tg, tb, db, ib, hg, hb = outs[4:-2]
     return (
         result, input_grad, fg, fb, dj, qb, vb, sg, sb, dout, ob, tg, tb, di, ib, hg, hb, dd, db,
     )

time: 232 us -> 167 us (0.72)
  Pallas kernels: 204 us -> 166 us
  local copies, waits for them, and re-layouts: 19.3 us -> 0 us
  other arithmetic: 7.81 us -> 0 us
    pallas_call x1, Pallas kernels: 196 us -> 135 us  [per_device(): pl.pallas_call(layer_kernel, out_shape=[shape((R, HD), BF16), shape((R, H...]
    pallas_call x1, Pallas kernels: 7.86 us -> 30.4 us  [per_device(): pl.pallas_call(finish_kernel, grid=(steps,), out_shape=[shape(s, F32) for...]
    reshape x10 -> x0, local copies, waits for them, and re-layouts: 12.7 us -> none  [per_device(): m.reshape(1, -1)]
    pallas_call x13 -> x0, other arithmetic: 7.81 us -> none  [per_device(): pl.pallas_call(finish_kernel, grid=(steps,), out_shape=[shape(s, F32) for...]
    unnamed x14 -> x0, local copies, waits for them, and re-layouts: 6.61 us -> none
where the time goes in v1:
time: 167 us
  Pallas kernels  166 us (99%)
    pallas_call x1, Pallas kernels, per_device(): pl.pallas_call(layer_kernel, out_shape=[shape((R, HD), BF16), shape((R, H...  135 us
    pallas_call x1, Pallas kernels, per_device(): pl.pallas_call(finish_kernel, grid=(steps,), out_shape=[shape(s, F32) for...  30.4 us

profile of v1, /device:TPU:1, one launch (start us, length us, event | category | flops | bytes accessed | tf_op | source)
XLA Modules:
  0.0 166.5 jit_solution(6797899389626890792)
XLA Ops:
  0.7 135.2 %shard_map.339 = (bf16[576,384]{1,0:T(8,128)(2,1)}, bf16[576,384]{1,0:T(8,128)(2,1)}, bf16[2,2,2,48,2304]{4,3,2,1,0:T(8,128)(2,1)}, bf16[2,2,2,48,768]{4,3,2,1,0...) custom-call(bf16[576,384]{1,0:T(8,128)(2,1)} %x_in.1, ...), custom_call_target="tpu_custom_call" | custom-call | flops 16000000000 | bytes 25000000 | tf_op jit(solution)/shard_map/pallas_call | solution.py:861
  135.9 30.4 %shard_map.340 = (f32[384,2304]{1,0:T(8,128)}, f32[384,768]{1,0:T(8,128)}, f32[384,3072]{1,0:T(8,128)}, f32[1536,768]{1,0:T(8,128)}, f32[384]{0:T(512)}, /*index...) custom-call(bf16[384,2304]{1,0:T(8,128)(2,1)} %bitcast.9, ...), custom_call_target="tpu_custom_call" | custom-call | tf_op jit(solution)/shard_map/pallas_call | solution.py:890

commit v2 on v1

--- a/solution.py
+++ b/solution.py
@@ -17,35 +17,35 @@
 PAIRS = HEADS // 4
 UNITS = 12
 AXES = ("x", "y", "a", "b")
-SUM_ORDER = ("axyb", "xyab", "yaxb", "aybx", "abxy", "yaxb", "xayb", "xyab", "yxab", "xyab", "yxab", "yxab")
-GATHER_ORDER = ("bay", "bay", "bay", "bay", "bya", "bay", "bay", "bay", "bya", "bay", "bya", "bay")
+SUM_ORDER = ("yaxb", "aybx", "yaxb", "xayb", "xyab", "yxab", "ayxb", "yxab", "xyab", "axyb", "xyab", "yxab")
+GATHER_ORDER = ("bay", "bay", "bay", "bay", "bay", "bay", "bay", "yba", "bay", "yba", "bay", "bay")
 SCHEDULE = (
     (0, ((0, 0),)),
     (1, ((1, 0),)),
-    (2, ((2, 0),)),
-    (3, ()),
-    ("result", ((3, 0),)),
+    (2, ()),
+    (3, ((3, 0),)),
+    ("result", ((2, 0),)),
     ("down_back0", ()),
-    ("down_back1", ((0, 1), (1, 1))),
-    ("down_back2", ((2, 1),)),
+    ("down_back1", ((0, 1),)),
+    ("down_back2", ((1, 1), (3, 1))),
     ("inner_back0", ()),
-    ("inner_back1", ()),
+    ("inner_back1", ((0, 2),)),
     ("gfn", ()),
-    ("handed", ((1, 2), (3, 1))),
-    ("mixed", ()),
-    (4, ((4, 0), (0, 2))),
-    (5, ((2, 2), (5, 0))),
+    ("handed", ((2, 1),)),
+    ("mixed", ((3, 2), (0, 3))),
+    (4, ((4, 0), (1, 2))),
+    (5, ((5, 0),)),
     (6, ((6, 0),)),
-    (7, ((1, 3), (3, 2))),
+    (7, ((3, 3), (2, 2))),
     (8, ()),
-    ("heads0", ((0, 3), (2, 3))),
-    ("heads1", ((7, 0), (8, 0))),
-    ("heads2", ((4, 1), (5, 1), (6, 1), (1, 4))),
-    (9, ((3, 3),)),
-    (10, ((0, 4), (10, 0))),
-    (11, ((2, 4), (9, 0))),
-    ("joint_back", ()),
-    ("end", ((8, 1), ("v", 0), (7, 1), (3, 4), ("v", 1), (5, 2), (4, 2), (11, 0), (6, 2), (10, 1), (1, 5), (9, 1), (0, 5), (2, 5), (3, 5), (7, 2), (1, 6), (0, 6), (2, 6), (3, 6), (8, 2), (11, 1), (7, 3), ("v", 2), (6, 3), (5, 3), (8, 3), (4, 3), (7, 4), (9, 2), (6, 4), (10, 2), (5, 4), (1, 7), (9, 3), (8, 4), (11, 2), (7, 5), (10, 3), (0, 7), (6, 5), (5, 5), (2, 7), (11, 3), (9, 4), (7, 6), (8, 5), (3, 7), (10, 4), (6, 6), ("v", 3), (4, 4), (5, 6), (11, 4), (9, 5), (7, 7), (10, 5), ("v", 4), (8, 6), (4, 5), (11, 5), (9, 6), (6, 7), ("v", 5), (5, 7), (8, 7), (10, 6), (11, 6), (4, 6), (9, 7), (10, 7), (11, 7), (4, 7))),
+    ("heads0", ((0, 4), (7, 0), (8, 0))),
+    ("heads1", ((1, 3),)),
+    ("heads2", ((2, 3), (5, 1), (4, 1))),
+    (9, ((9, 0),)),
+    (10, ((6, 1),)),
+    (11, ((3, 4),)),
+    ("joint_back", ((0, 5), (2, 4), (10, 0))),
+    ("end", (("v", 0), (7, 1), (1, 4), (11, 0), (8, 1), ("v", 1), (4, 2), (9, 1), (5, 2), (3, 5), (6, 2), (0, 6), (2, 5), (1, 5), (4, 3), (10, 1), (5, 3), (11, 1), (3, 6), (2, 6), (8, 2), (1, 6), (4, 4), (5, 4), (7, 2), (0, 7), (8, 3), ("v", 2), (4, 5), (10, 2), (7, 3), (5, 5), (9, 2), (8, 4), (4, 6), (6, 3), (3, 7), (10, 3), (7, 4), (11, 2), (2, 7), (5, 6), (8, 5), (6, 4), (1, 7), (10, 4), (11, 3), ("v", 3), (8, 6), (9, 3), (6, 5), (10, 5), (4, 7), (11, 4), ("v", 4), (7, 5), (9, 4), (6, 6), (5, 7), (10, 6), (11, 5), (8, 7), ("v", 5), (9, 5), (11, 6), (7, 6), (6, 7), (9, 6), (10, 7), (7, 7), (11, 7), (9, 7))),
 )
 GELU_C = 0.7978845608028654
 GELU_A = 0.044715
@@ -181,14 +181,16 @@
 
 def layer_kernel(
     x_in, cot_in, lens, wj_in, wo_in, wi_in, wd_in,
-    first_gain, first_bias, query_bias, value_bias, second_gain, second_bias, output_bias,
-    third_gain, third_bias, down_bias, inner_bias, fourth_gain, fourth_bias,
+    *rest,
+):
+    lines, rest = rest[:13], rest[13:]
+    (
     res_out, grad_out, gj_out, go_out, gi_out, gd_out, bv_out,
-    wj, wo, wi, wd, feats, cots, ends, normed, q, k, v, vt, kt, bias, pt, mixed_own, mixed,
-    sub, fn, handed, tmp, vh, dg, fs, fs_sib, gi_sib, up, gfn, hgr, hg_sib, gmix, do, dqkv,
+    wj, wo, wi, wd, feats, cots, ends, normed, q, k, v, vt, kt, bias, pt, scales, mixed_own, mixed,
+    sub, fn, handed, tmp, vh, pre, fs, fs_sib, gi_sib, up, gfn, hgr, hg_sib, gmix, do, dqkv,
     result, stat, cols, bv, bv_in, grads, r1, r2, r3, r4, whole,
-    vectors, lsem, ssem, rsem,
-):
+    vectors, inner_bias, fourth_gain, fourth_bias, *line_refs, lsem, ssem, rsem,
+    ) = rest
     R, HD = x_in.shape
     D = 2 * HD
     H = R // 2
@@ -225,25 +227,25 @@
         copy.start()
         return copy
 
-    wj_copies = [local(wj_in.at[:, pl.ds(aligned(t * D + c * HD, 128), HD)], wj.at[t]) for t in range(3)]
-    wo_copy = local(wo_in, wo)
-    wi_copy = local(wi_in, wi)
-    wd_copy = local(wd_in, wd)
-
-    lines = (
-        first_gain, first_bias, query_bias, value_bias, second_gain, second_bias, output_bias,
-        third_gain, third_bias, down_bias,
-    )
-    for i, line in enumerate(lines):
-        vectors[i : i + 1, :] = line[...].reshape(1, D)
+    barrier = pltpu.get_barrier_semaphore()
+    for peer in (*peers.values(), xc):
+        pl.semaphore_signal(barrier, inc=1, device_id=peer, device_id_type=MESH)
+
+    line_refs += [inner_bias, fourth_gain, fourth_bias]
+    line_copies = [local(src, dst) for src, dst in zip(lines, line_refs)]
     (
         first_gain, first_bias, query_bias, value_bias, second_gain, second_bias, output_bias,
         third_gain, third_bias, down_bias,
-    ) = (vectors.at[i : i + 1] for i in range(len(lines)))
-
-    barrier = pltpu.get_barrier_semaphore()
-    for peer in (*peers.values(), xc):
-        pl.semaphore_signal(barrier, inc=1, device_id=peer, device_id_type=MESH)
+    ) = (vectors.at[i : i + 1] for i in range(10))
+
+    @pl.when(home)
+    def _():
+        lane = lax.broadcasted_iota(jnp.int32, (1, 8), 1)
+        lengths = lens[...].astype(F32)
+        for j in range(8):
+            end = jnp.sum(jnp.where(lane <= j, lengths, 0.0), axis=1, keepdims=True)
+            ends[j : j + 1, :] = jnp.broadcast_to(end, (1, 128))
+
     pl.semaphore_wait(barrier, 6)
 
     NC = 3
@@ -260,35 +262,38 @@
     cot_cross = cp.remote(cot_in, cots.at[x], xp)
     cot_pass = cp.remote(cots.at[1 - x], cots.at[1 - x], sib)
     l_native = [
-        pltpu.make_async_copy(src, dst.at[x], lsem.at[12 + i])
+        pltpu.make_async_copy(src, dst.at[x], lsem.at[44 + i])
         for i, (src, dst) in enumerate(((x_in, feats), (cot_in, cots)))
     ]
 
     @pl.when(away)
     def _():
-        for copy in c_cross:
-            copy.start()
-        cot_cross.start()
+        c_cross[0].start()
+        c_cross[1].start()
 
     @pl.when(home)
     def _():
         c_native[0].start()
         l_native[0].start()
-        lane = lax.broadcasted_iota(jnp.int32, (1, 8), 1)
-        lengths = lens[...].astype(F32)
-        for j in range(8):
-            end = jnp.sum(jnp.where(lane <= j, lengths, 0.0), axis=1, keepdims=True)
-            ends[j : j + 1, :] = jnp.broadcast_to(end, (1, 128))
         c_ends.start()
         l_native[1].start()
         c_native[1].start()
         l_native[0].wait()
 
+    wj_copies = [local(wj_in.at[:, pl.ds(aligned(t * D + c * HD, 128), HD)], wj.at[t]) for t in range(3)]
+    wo_copy = local(wo_in, wo)
+    wi_copy = local(wi_in, wi)
+    wd_copy = local(wd_in, wd)
+
     @pl.when(away)
     def _():
         c_native[0].wait_recv()
         c_ends.wait_recv()
 
+    for copy in line_copies:
+        copy.wait()
+    for i in range(10):
+        vectors[i : i + 1, :] = line_refs[i][...].reshape(1, D)
     zeros = jnp.zeros((640 - R, HD), BF16)
     for ref in (q, do):
         ref[R:640, :] = zeros
@@ -318,6 +323,13 @@
 
         @pl.when(away)
         def _():
+            if i == 0:
+                c_cross[0].wait_send()
+                c_cross[2].start()
+            if i == 1:
+                c_cross[1].wait_send()
+                c_cross[2].wait_send()
+                cot_cross.start()
             c_pass[i].wait_recv()
 
         @pl.loop(0, RC // 48)
@@ -344,6 +356,7 @@
     for j in range(5):
         blocks.append((j, min(128 * (j + 1), R), at))
         at += min(128 * (j + 1), R)
+    c_mixed = []
     for pr in range(PAIRS):
         lanes = slice(pr * 128, (pr + 1) * 128)
         for j, nk, at in blocks:
@@ -354,18 +367,44 @@
             largest = jnp.max(scores, axis=0, keepdims=True)
             shifted = jnp.exp(scores - largest)
             summed = jnp.sum(shifted, axis=0, keepdims=True)
-            probs = (shifted * (1.0 / summed)).astype(BF16)
-            pt[pr, at : at + nk, :] = probs
-            out = dot(vt[lanes, :nk], probs)
+            scale = 1.0 / summed
+            weights = shifted.astype(BF16)
+            pt[pr, at : at + nk, :] = weights
+            scales[pr * 5 + j] = jnp.broadcast_to(scale, (8, 256))
+            out = dot(vt[lanes, :nk], weights) * scale
             mixed_own[qs, lanes] = jnp.concatenate([out[:64, :128], out[64:, 128:]], 0).T
-
-    c_mixed = cp.go(
-        mixed_own.at[pl.ds(other, H)], mixed.at[:, pl.ds(heads_at, HD)], sib
-    )
-    mixed[:, pl.ds(heads_at, HD)] = mixed_own[pl.ds(own, H), :]
+        there = pl.ds(aligned(c * HD + pr * 128, 128), 128)
+        c_mixed.append(cp.go(mixed_own.at[pl.ds(other, H), lanes], mixed.at[:, there], sib))
+        mixed[:, there] = mixed_own[pl.ds(own, H), lanes]
+
     kt[:, :R] = k[...].T
+
+    @pl.when(home)
+    def _():
+        cot_cross.wait_recv()
+        cot_pass.start()
+        l_native[1].wait()
+        cot_pass.wait_send()
+
+    @pl.when(away)
+    def _():
+        c_native[1].wait_recv()
+        cot_pass.wait_recv()
+
+    @pl.loop(0, R // 48)
+    def _(step):
+        at = aligned(step * 48, 16)
+        alive = (lax.broadcasted_iota(jnp.int32, (48, 1), 0) + at).astype(F32) < ends[7:8, 0:1]
+        for h in range(2):
+            rows = cots[h, pl.ds(at, 48), :].astype(F32)
+            cots[h, pl.ds(at, 48), :] = jnp.where(alive, rows, 0.0).astype(BF16)
+
+    up[:, :HD] = cots[0, pl.ds(own, H), :]
+    up[:, HD:] = cots[1, pl.ds(own, H), :]
+
     wo_copy.wait()
-    c_mixed.wait_recv()
+    for copy in c_mixed:
+        copy.wait_recv()
     own_live = (lax.broadcasted_iota(jnp.int32, (H, 1), 0) + c * H).astype(F32) < ends[7:8, 0:1]
 
     @pl.loop(0, H // 48)
@@ -386,84 +425,73 @@
     c_fn = cp.go(fn.at[pl.ds(own, H)], fn.at[pl.ds(own, H)], sib)
 
     wi_copy.wait()
-    stat[0] = jnp.zeros((H, 128), F32)
-
-    @pl.loop(0, NT)
-    def _(tile):
+
+    def feed_dot(tile):
         at = pl.ds(aligned(tile * T, T), T)
-        inner = dot(fn[pl.ds(own, H), :], wi[:, at])
-        for i in range(9):
-            piece = slice(i * 32, (i + 1) * 32)
-            u = inner[piece] + inner_bias[:, at]
-            square = u * u
-            t = jnp.tanh(u * (GELU_C + (GELU_C * GELU_A) * square))
-            half = 0.5 * u
-            act = half + half * t
-            tmp[piece, at] = act
-            dg[piece, at] = (
-                0.5 + 0.5 * t + (half - half * t * t) * (GELU_C + (3 * GELU_C * GELU_A) * square)
-            ).astype(BF16)
-            stat[0, piece, :] += act[:, :128] + act[:, 128:]
-
-    mean = jnp.sum(stat[0], axis=1, keepdims=True) * (1.0 / FF)
-    stat[1] = jnp.broadcast_to(mean, (H, 128))
-    stat[0] = jnp.zeros((H, 128), F32)
-
-    @pl.loop(0, NT)
-    def _(tile):
+        tmp[:, at] = dot(fn[pl.ds(own, H), :], wi[:, at])
+
+    def feed_tile(tile, first=False):
         at = pl.ds(aligned(tile * T, T), T)
         for i in range(9):
             piece = slice(i * 32, (i + 1) * 32)
-            m = stat[1, piece, :]
-            cen = tmp[piece, at] - jnp.concatenate([m, m], 1)
-            sq = cen * cen
-            stat[0, piece, :] += sq[:, :128] + sq[:, 128:]
-
-    spread = jnp.sum(stat[0], axis=1, keepdims=True) * (1.0 / FF)
-    stat[2] = jnp.broadcast_to(lax.rsqrt(spread + EPSILON), (H, 128))
-
-    @pl.loop(0, NT)
+            u = tmp[piece, at] + inner_bias[:, at]
+            pre[piece, at] = u.astype(BF16)
+            half = 0.5 * u
+            act = half + half * jnp.tanh(u * (GELU_C + (GELU_C * GELU_A) * (u * u)))
+            tmp[piece, at] = act
+            if first:
+                near = jnp.sum(act, axis=1, keepdims=True) * (1.0 / T)
+                stat[1, piece, :] = jnp.broadcast_to(near, (32, 128))
+            near = stat[1, piece, :]
+            low, high = act[:, :128] - near, act[:, 128:] - near
+            if first:
+                stat[0, piece, :] = low + high
+                stat[2, piece, :] = low * low + high * high
+            else:
+                stat[0, piece, :] += low + high
+                stat[2, piece, :] += low * low + high * high
+
+    feed_dot(0)
+    feed_dot(1)
+    feed_tile(0, True)
+
+    @pl.loop(1, NT - 1)
     def _(tile):
-        at = pl.ds(aligned(tile * T, T), T)
+        feed_dot(tile + 1)
+        feed_tile(tile)
+
+    feed_tile(NT - 1)
+    shift = jnp.sum(stat[0], axis=1, keepdims=True) * (1.0 / FF)
+    spread = jnp.sum(stat[2], axis=1, keepdims=True) * (1.0 / FF) - shift * shift
+    stat[1] = stat[1] + shift
+    stat[2] = jnp.broadcast_to(lax.rsqrt(jnp.maximum(spread, 0.0) + EPSILON), (H, 128))
+
+    def feed_norm(block):
+        at = pl.ds(aligned(block * HD, HD), HD)
         for i in range(9):
             piece = slice(i * 32, (i + 1) * 32)
             m, s = stat[1, piece, :], stat[2, piece, :]
-            vhat = (tmp[piece, at] - jnp.concatenate([m, m], 1)) * jnp.concatenate([s, s], 1)
+            vhat = (tmp[piece, at] - jnp.concatenate([m, m, m], 1)) * jnp.concatenate([s, s, s], 1)
             vh[piece, at] = vhat.astype(BF16)
             fs[piece, at] = (vhat * fourth_gain[:, at] + fourth_bias[:, at]).astype(BF16)
 
-    c_fs = [
-        cp.go(
-            fs.at[:, pl.ds(aligned((2 * i + 1 - c) * D, 128), D)],
-            fs_sib.at[:, i * D : (i + 1) * D],
-            sib,
-            keep=False,
-        )
-        for i in range(2)
-    ]
-
-    @pl.when(home)
-    def _():
-        cot_cross.wait_recv()
-        cot_pass.start()
-        l_native[1].wait()
-        cot_pass.wait_send()
-
-    @pl.when(away)
-    def _():
-        c_native[1].wait_recv()
-        cot_pass.wait_recv()
-
-    @pl.loop(0, R // 48)
+    c_fs = []
+    for part in range(2):
+        for i in range(2):
+            feed_norm(4 * i + 2 * (1 - c) + part)
+        for i in range(2):
+            c_fs.append(
+                cp.go(
+                    fs.at[:, pl.ds(aligned((4 * i + 2 * (1 - c) + part) * HD, 128), HD)],
+                    fs_sib.at[:, (2 * i + part) * HD : (2 * i + part + 1) * HD],
+                    sib,
+                    keep=False,
+                )
+            )
+
+    @pl.loop(0, 4)
     def _(step):
-        at = aligned(step * 48, 16)
-        alive = (lax.broadcasted_iota(jnp.int32, (48, 1), 0) + at).astype(F32) < ends[7:8, 0:1]
-        for h in range(2):
-            rows = cots[h, pl.ds(at, 48), :].astype(F32)
-            cots[h, pl.ds(at, 48), :] = jnp.where(alive, rows, 0.0).astype(BF16)
-
-    up[:, :HD] = cots[0, pl.ds(own, H), :]
-    up[:, HD:] = cots[1, pl.ds(own, H), :]
+        feed_norm((step // 2) * 4 + 2 * c + step % 2)
 
     deliveries = []
 
@@ -498,13 +526,14 @@
 
     def units(first, count, left_own, left_sib, right):
         for i in range(count):
+            if first == 0 and i % 2 == 0:
+                c_fs[i].wait_recv()
+                c_fs[i + 1].wait_recv()
             for h in range(2):
                 rows = jnp.concatenate([left_own(i, h), left_sib(i, h)], 0)
                 grads[first + i, h] = cut_rows(t_dot(rows, right(i)))
             pump(first + i)
 
-    for copy in c_fs:
-        copy.wait_recv()
     units(
         0, 4,
         lambda i, h: fs[:, pl.ds(aligned((2 * h + c) * D + (i // 2) * HD, 128), HD)],
@@ -522,7 +551,7 @@
         cp.remote(result.at[1, 1 - x], grad_out.at[pl.ds(own, H)], xc),
     ]
     l_result = [
-        pltpu.make_async_copy(result.at[i, x], o.at[pl.ds(own, H)], lsem.at[14 + i])
+        pltpu.make_async_copy(result.at[i, x], o.at[pl.ds(own, H)], lsem.at[46 + i])
         for i, o in enumerate((res_out, grad_out))
     ]
 
@@ -605,7 +634,14 @@
             vhat = vh[piece, at].astype(F32)
             grad = tmp[piece, at] * fourth_gain[:, at] - jnp.concatenate([m1, m1], 1)
             grad = (grad - vhat * jnp.concatenate([m2, m2], 1)) * jnp.concatenate([s, s], 1)
-            low = (grad * dg[piece, at].astype(F32)).astype(BF16)
+            u = pre[piece, at].astype(F32)
+            square = u * u
+            t = jnp.tanh(u * (GELU_C + (GELU_C * GELU_A) * square))
+            half = 0.5 * u
+            slope = 0.5 + 0.5 * t + (half - half * t * t) * (
+                GELU_C + (3 * GELU_C * GELU_A) * square
+            )
+            low = (grad * slope).astype(BF16)
             gi[piece, at] = low
             total += by8(low.astype(F32))
         cols[2, tile] = total
@@ -690,10 +726,10 @@
         lanes = slice(pr * 128, (pr + 1) * 128)
         for j, nk, at in reversed(blocks):
             qs = slice(j * 128, (j + 1) * 128)
-            probs = pt[pr, at : at + nk, :]
+            exact = pt[pr, at : at + nk, :].astype(F32) * scales[pr * 5 + j][:1]
+            probs = exact.astype(BF16)
             do_split = split_pair(do[qs, lanes])
             grad_probs = dot_t(v[:nk, lanes], do_split)
-            exact = probs.astype(F32)
             inner_sum = jnp.sum(exact * grad_probs, axis=0, keepdims=True)
             grad_scores = (exact * (grad_probs - inner_sum)).astype(BF16)
             value_part = dot(probs, do_split)
@@ -780,8 +816,7 @@
 
     @pl.when(away)
     def _():
-        for copy in c_cross + [cot_cross]:
-            copy.wait_send()
+        cot_cross.wait_send()
 
     handed_out(0)
     handed_out(1)
@@ -793,13 +828,10 @@
 
 
 def finish_kernel(gj, go, gi, gd, bv, res, grad, oj, oo, oi, od, *rest):
-    *vectors, res_out, grad_out, sem = rest
-    copies = [pltpu.make_async_copy(res, res_out, sem.at[0]), pltpu.make_async_copy(grad, grad_out, sem.at[1])]
+    *vectors, res_out, grad_out = rest
 
     @pl.when(pl.program_id(0) == 0)
     def _():
-        for copy in copies:
-            copy.start()
         x = lax.axis_index("section")
         HD = oo.shape[1] // 2
         at = pl.ds(aligned(x * HD, 128), HD)
@@ -815,10 +847,8 @@
     oi[...] = gi[...].astype(F32)
     od[...] = gd[...].astype(F32)
 
-    @pl.when(pl.program_id(0) == pl.num_programs(0) - 1)
-    def _():
-        for copy in copies:
-            copy.wait()
+    res_out[...] = res[...]
+    grad_out[...] = grad[...]
 
 
 def per_device(
@@ -842,7 +872,7 @@
         V((2, R, HD), BF16), V((2, R, HD), BF16), V((8, 128), F32), V((R, D), BF16),
         V((640, HD), BF16), V((R, HD), BF16), V((R, HD), BF16),
         V((HD, 640), BF16), V((HD, 640), BF16), V((R, 640), BF16),
-        V((PAIRS, 128 * 10 + R, 256), BF16),
+        V((PAIRS, 128 * 10 + R, 256), BF16), V((PAIRS * 5, 8, 256), F32),
         V((640, HD), F32), V((H, D), F32),
         V((R, D), BF16), V((R, D), BF16), V((H, D), BF16),
         V((H, FF), F32), V((H, FF), BF16), V((H, FF), BF16),
@@ -855,7 +885,8 @@
         V((UNITS, 2, 2, 2, HD // 8, HD), BF16), V((UNITS, 2, 2, HD // 8, HD), BF16),
         V((UNITS, 2, HD // 8, HD), BF16), V((UNITS, HD // 8, HD), BF16),
         V((UNITS, 2, 2, 2, HD // 8, HD), BF16),
-        V((10, D), F32), pltpu.SemaphoreType.DMA((32,)), pltpu.SemaphoreType.DMA((200,)), pltpu.SemaphoreType.DMA((200,)),
+        V((10, D), F32), *[V((1, FF), F32)] * 3, *[V((D,), F32)] * 10,
+        pltpu.SemaphoreType.DMA((48,)), pltpu.SemaphoreType.DMA((200,)), pltpu.SemaphoreType.DMA((200,)),
     ]
     shape = jax.ShapeDtypeStruct
     result, input_grad, gj, go, gi, gd, bv = pl.pallas_call(
@@ -865,7 +896,7 @@
             *(shape((2, 2, 2, HD // 8, n), BF16) for n in (3 * D, D, FF)),
             shape((2, 2, 2, 2, 2, HD // 8, D), BF16), shape((24, D), F32),
         ],
-        in_specs=[hbm, hbm, vmem, hbm, hbm, hbm, hbm] + [vmem] * 13,
+        in_specs=[hbm, hbm, vmem, hbm, hbm, hbm, hbm] + [hbm] * 13,
         out_specs=[hbm] * 7,
         scratch_shapes=scratch,
         compiler_params=pltpu.CompilerParams(
@@ -873,7 +904,7 @@
         ),
         cost_estimate=pl.CostEstimate(flops=16 * 10**9, bytes_accessed=25 * 10**6, transcendentals=4 * 10**6),
     )(inputs, cotangent, seq_lengths, joint_weight, output_weight, inner_weight, down_weight, *lines)
-    steps = 8
+    steps = 2
     wide = [(HD, 3 * D), (HD, D), (HD, FF), (FF // 2, D)]
     gj, go, gi, gd = (m.reshape(s) for m, s in zip((gj, go, gi, gd), wide))
 
@@ -891,9 +922,8 @@
         finish_kernel,
         grid=(steps,),
         out_shape=[shape(s, F32) for s in wide + small] + [shape((R, HD), BF16)] * 2,
-        in_specs=[block(*s) for s in wide] + [pl.BlockSpec((24, D), lambda i: (0, 0)), hbm, hbm],
-        out_specs=[block(*s) for s in wide] + [pl.BlockSpec(s, lambda i: (0,)) for s in small] + [hbm, hbm],
-        scratch_shapes=[pltpu.SemaphoreType.DMA((2,))],
+        in_specs=[block(*s) for s in wide] + [pl.BlockSpec((24, D), lambda i: (0, 0))] + [block(R, HD)] * 2,
+        out_specs=[block(*s) for s in wide] + [pl.BlockSpec(s, lambda i: (0,)) for s in small] + [block(R, HD)] * 2,
         compiler_params=pltpu.CompilerParams(vmem_limit_bytes=66_000_000),
     )(gj, go, gi, gd, bv, result, input_grad)
     result, input_grad = outs[-2:]

time: 167 us -> 139 us (0.83)
  Pallas kernels: 166 us -> 138 us
    pallas_call x1, Pallas kernels: 30.4 us -> 8.43 us  [per_device(): pl.pallas_call(finish_kernel, grid=(steps,), out_shape=[shape(s, F32) for...]
    pallas_call x1, Pallas kernels: 135 us -> 130 us  [per_device(): pl.pallas_call(layer_kernel, out_shape=[shape((R, HD), BF16), shape((R, H...]
where the time goes in v2:
time: 139 us
  Pallas kernels  138 us (99%)
    pallas_call x1, Pallas kernels, per_device(): pl.pallas_call(layer_kernel, out_shape=[shape((R, HD), BF16), shape((R, H...  130 us
    pallas_call x1, Pallas kernels, per_device(): pl.pallas_call(finish_kernel, grid=(steps,), out_shape=[shape(s, F32) for...  8.43 us

profile of v2, /device:TPU:1, one launch (start us, length us, event | category | flops | bytes accessed | tf_op | source)
XLA Modules:
  0.0 139.2 jit_solution(3229310910775323631)
XLA Ops:
  0.7 130.0 %shard_map.339 = (bf16[576,384]{1,0:T(8,128)(2,1)}, bf16[576,384]{1,0:T(8,128)(2,1)}, bf16[2,2,2,48,2304]{4,3,2,1,0:T(8,128)(2,1)}, bf16[2,2,2,48,768]{4,3,2,1,0...) custom-call(bf16[576,384]{1,0:T(8,128)(2,1)} %x_in.1, ...), custom_call_target="tpu_custom_call" | custom-call | flops 16000000000 | bytes 25000000 | tf_op jit(solution)/shard_map/pallas_call | solution.py:892
  130.6 8.4 %shard_map.340 = (f32[384,2304]{1,0:T(8,128)}, f32[384,768]{1,0:T(8,128)}, f32[384,3072]{1,0:T(8,128)}, f32[1536,768]{1,0:T(8,128)}, f32[384]{0:T(512)}, /*index...) custom-call(bf16[384,2304]{1,0:T(8,128)(2,1)} %bitcast.9, ...), custom_call_target="tpu_custom_call" | custom-call | tf_op jit(solution)/shard_map/pallas_call | solution.py:921
